TPU v7x, 512 devices: a whole 4x8x8 slice. The times are simulated.
512 devices in a mesh: ep: 128 (over y, z, core), dp: 4 (over x).
Axes of the slice: x: 4, y: 8, z: 8, core: 2. Of those that a mesh axis runs over, the one named last changes fastest.
Arguments:
- tokens: bfloat16 [65536, 1024], P(('ep', 'dp')), may hold values from -6 to 6
- expert_ids: int32 [65536, 8], P(('ep', 'dp')), may hold values from 0 to 127, all different within a row; in each aligned block of 128 rows (0 to 127, 128 to 255, ...) at most 10 rows name the same one
- gate_weights: bfloat16 [65536, 8], P(('ep', 'dp')), may hold values from 0.049804688 to 0.25
- cotangent: bfloat16 [65536, 1024], P(('ep', 'dp')), may hold values from -6 to 6
- migration_plan: int32 [8, 2], replicated, may hold values from 0 to 127, as said below
- master: float32 [128, 2, 1024, 384], P('ep', None, 'dp'), may hold values from -0.1875 to 0.1875
- moment_one: bfloat16 [128, 2, 1024, 384], P('ep', None, 'dp'), may hold values from -12 to 12
- moment_two: bfloat16 [128, 2, 1024, 384], P('ep', None, 'dp'), may hold values from 1 to 16
- average: bfloat16 [128, 2, 1024, 384], P('ep', None, 'dp'), may hold values from -0.1875 to 0.1875
Outputs:
- token_grad: bfloat16 [65536, 1024], P(('ep', 'dp'))
- gate_grad: bfloat16 [65536, 8], P(('ep', 'dp'))
- new_master: float32 [128, 2, 1024, 384], P('ep', None, 'dp')
- new_moment_one: bfloat16 [128, 2, 1024, 384], P('ep', None, 'dp')
- new_moment_two: bfloat16 [128, 2, 1024, 384], P('ep', None, 'dp')
- new_average: bfloat16 [128, 2, 1024, 384], P('ep', None, 'dp')
Inputs may be any that keep to these rules, and one draw needn't show every extreme that they name: `expert_ids`: each row names 8 different experts. Within the rows of one device no expert is named more than 10 times, a bound that some block reaches. `migration_plan`: the 16 entries are all different.
All inputs are finite; a program needn't handle non-finite values.
Results may differ from a plain program's by a relative error of at most 0.015.
Values may be sent and summed in bfloat16 or wider, within the bound.
A program may use at most 128 MiB of HBM per device.

v0:
```python
import jax
import jax.numpy as jnp
from jax import lax
from jax.sharding import PartitionSpec as P

LEARN_RATE = 0.01
BETA_ONE = 0.9
BETA_TWO = 0.95
ADAM_EPS = 1e-08
EMA_DECAY = 0.99


def holders(migration_plan, count):
    mapping = jnp.arange(count, dtype=jnp.int32)
    mapping = mapping.at[migration_plan[:, 1]].set(migration_plan[:, 0])
    return mapping.at[migration_plan[:, 0]].set(migration_plan[:, 1])


def expert_forward(received_rows, up_proj, down_proj):
    activation = jnp.dot(received_rows, up_proj, preferred_element_type=jnp.float32)
    gate_sigma = jax.nn.sigmoid(activation)
    hidden = (activation * gate_sigma).astype(jnp.bfloat16)
    output = lax.dot_general(
        hidden, down_proj, (((1,), (1,)), ((), ())), preferred_element_type=jnp.float32
    )
    return (activation, gate_sigma, hidden, output)


def expert_backward(
    received_rows,
    received_cotan,
    weight,
    up_proj,
    down_proj,
    activation,
    gate_sigma,
    hidden,
    output,
):
    gate_grad = jnp.sum(received_cotan.astype(jnp.float32) * output, axis=1).astype(jnp.bfloat16)
    scaled = (weight.astype(jnp.float32)[:, None] * received_cotan.astype(jnp.float32)).astype(
        jnp.bfloat16
    )
    hidden_grad = jnp.dot(scaled, down_proj, preferred_element_type=jnp.float32)
    activation_grad = (hidden_grad * gate_sigma * (1.0 + activation * (1.0 - gate_sigma))).astype(
        jnp.bfloat16
    )
    pair_grad = lax.dot_general(
        activation_grad, up_proj, (((1,), (1,)), ((), ())), preferred_element_type=jnp.float32
    ).astype(jnp.bfloat16)
    up_grad = lax.dot_general(
        received_rows, activation_grad, (((0,), (0,)), ((), ())), preferred_element_type=jnp.float32
    )
    down_grad = lax.dot_general(
        scaled, hidden, (((0,), (0,)), ((), ())), preferred_element_type=jnp.float32
    )
    return (gate_grad, pair_grad, up_grad, down_grad)


def adam_update(master, moment_one, moment_two, average, gradient):
    first_moment = BETA_ONE * moment_one.astype(jnp.float32) + (1.0 - BETA_ONE) * gradient
    second_moment = (
        BETA_TWO * moment_two.astype(jnp.float32) + (1.0 - BETA_TWO) * gradient * gradient
    )
    new_master = master - LEARN_RATE * first_moment / (jnp.sqrt(second_moment) + ADAM_EPS)
    smoothed = EMA_DECAY * average.astype(jnp.float32) + (1.0 - EMA_DECAY) * new_master
    return (
        new_master,
        first_moment.astype(jnp.bfloat16),
        second_moment.astype(jnp.bfloat16),
        smoothed.astype(jnp.bfloat16),
    )


def relocate_master(master, holder):
    state_shape = master.shape
    flattened = master.reshape(holder.shape[0], -1)
    pieces = lax.all_to_all(flattened, "ep", split_axis=0, concat_axis=0, tiled=True)
    arranged = jnp.take(pieces, holder, axis=0)
    returned = lax.all_to_all(arranged, "ep", split_axis=0, concat_axis=0, tiled=True)
    return returned.reshape(state_shape)


def relocate_moments(moment_one, moment_two, average, holder):
    state_shape = moment_one.shape
    peer_count = holder.shape[0]
    first_flat = moment_one.reshape(peer_count, -1)
    second_flat = moment_two.reshape(peer_count, -1)
    average_flat = average.reshape(peer_count, -1)
    first_pieces, second_pieces, average_pieces = (
        lax.all_to_all(first_flat, "ep", split_axis=0, concat_axis=0, tiled=True),
        lax.all_to_all(second_flat, "ep", split_axis=0, concat_axis=0, tiled=True),
        lax.all_to_all(average_flat, "ep", split_axis=0, concat_axis=0, tiled=True),
    )
    first_arranged = jnp.take(first_pieces, holder, axis=0)
    second_arranged = jnp.take(second_pieces, holder, axis=0)
    average_arranged = jnp.take(average_pieces, holder, axis=0)
    first_back, second_back, average_back = (
        lax.all_to_all(first_arranged, "ep", split_axis=0, concat_axis=0, tiled=True),
        lax.all_to_all(second_arranged, "ep", split_axis=0, concat_axis=0, tiled=True),
        lax.all_to_all(average_arranged, "ep", split_axis=0, concat_axis=0, tiled=True),
    )
    return (
        first_back.reshape(state_shape),
        second_back.reshape(state_shape),
        average_back.reshape(state_shape),
    )


def slot_plan(expert_ids, owners, peer_count, capacity):
    pair_experts = expert_ids.reshape(-1)
    pair_count = pair_experts.shape[0]
    columns = jnp.arange(owners.shape[0], dtype=jnp.int32)
    target = jnp.sum(
        jnp.where(pair_experts[:, None] == columns[None, :], owners[None, :], 0), axis=1
    )
    matches = target[:, None] == jnp.arange(peer_count, dtype=jnp.int32)[None, :]
    row_iota = lax.broadcasted_iota(jnp.int32, (pair_count, pair_count), 0)
    col_iota = lax.broadcasted_iota(jnp.int32, (pair_count, pair_count), 1)
    lower = (col_iota < row_iota).astype(jnp.bfloat16)
    earlier = jnp.dot(lower, matches.astype(jnp.bfloat16), preferred_element_type=jnp.float32)
    position = jnp.sum(jnp.where(matches, earlier, 0.0), axis=1).astype(jnp.int32)
    slot_index = target * capacity + position
    filler = (
        jnp.zeros((peer_count * capacity,), jnp.int32)
        .at[slot_index]
        .set(jnp.arange(pair_count, dtype=jnp.int32) + 1)
    )
    return (slot_index, filler)


def shards(
    tokens,
    expert_ids,
    gate_weights,
    cotangent,
    migration_plan,
    master,
    moment_one,
    moment_two,
    average,
):
    peer_count = lax.axis_size("ep")
    tok_rows = tokens.shape[0]
    top_count = expert_ids.shape[1]
    capacity = max(
        2, min(tok_rows, (5 * tok_rows * top_count + 4 * peer_count - 1) // (4 * peer_count))
    )
    holder = holders(migration_plan, peer_count)
    master_here = relocate_master(master, holder)
    moment_one, moment_two, average = relocate_moments(moment_one, moment_two, average, holder)
    gathered = lax.all_gather(master_here.astype(jnp.bfloat16), "dp", axis=2, tiled=True)
    up_proj = gathered[0, 0]
    down_proj = gathered[0, 1]
    slot_index, filler = slot_plan(expert_ids, holder, peer_count, capacity)
    filled = filler > 0
    pair_index = jnp.maximum(filler - 1, 0)
    token_index = pair_index // top_count
    send_rows = jnp.where(
        filled[:, None], jnp.take(tokens, token_index, axis=0), jnp.zeros((), jnp.bfloat16)
    )
    send_cotan = jnp.where(
        filled[:, None], jnp.take(cotangent, token_index, axis=0), jnp.zeros((), jnp.bfloat16)
    )
    send_weight = jnp.where(
        filled, jnp.take(gate_weights.reshape(-1), pair_index), jnp.zeros((), jnp.bfloat16)
    )
    received_rows, received_cotan, weight = (
        lax.all_to_all(send_rows, "ep", split_axis=0, concat_axis=0, tiled=True),
        lax.all_to_all(send_cotan, "ep", split_axis=0, concat_axis=0, tiled=True),
        lax.all_to_all(send_weight, "ep", split_axis=0, concat_axis=0, tiled=True),
    )
    activation, gate_sigma, hidden, output = expert_forward(received_rows, up_proj, down_proj)
    gate_slots, pair_grad, up_grad, down_grad = expert_backward(
        received_rows,
        received_cotan,
        weight,
        up_proj,
        down_proj,
        activation,
        gate_sigma,
        hidden,
        output,
    )
    back_rows, back_gates = (
        lax.all_to_all(pair_grad, "ep", split_axis=0, concat_axis=0, tiled=True),
        lax.all_to_all(gate_slots, "ep", split_axis=0, concat_axis=0, tiled=True),
    )
    grad_local = jnp.stack([up_grad, down_grad])[None]
    grad_share = lax.psum_scatter(
        grad_local.astype(jnp.bfloat16), "dp", scatter_dimension=2, tiled=True
    ).astype(jnp.float32)
    new_master, first_moment, second_moment, smoothed = adam_update(
        master_here, moment_one, moment_two, average, grad_share
    )
    pair_values = jnp.take(back_rows, slot_index, axis=0).reshape(tok_rows, top_count, -1)
    token_grad = jnp.sum(pair_values.astype(jnp.float32), axis=1).astype(jnp.bfloat16)
    gate_grad = jnp.take(back_gates, slot_index).reshape(tok_rows, top_count)
    return (token_grad, gate_grad, new_master, first_moment, second_moment, smoothed)


def solution(mesh):
    return jax.shard_map(
        shards,
        mesh=mesh,
        in_specs=(
            P(("ep", "dp"), None),
            P(("ep", "dp"), None),
            P(("ep", "dp"), None),
            P(("ep", "dp"), None),
            P(),
            P("ep", None, "dp", None),
            P("ep", None, "dp", None),
            P("ep", None, "dp", None),
            P("ep", None, "dp", None),
        ),
        out_specs=(
            P(("ep", "dp"), None),
            P(("ep", "dp"), None),
            P("ep", None, "dp", None),
            P("ep", None, "dp", None),
            P("ep", None, "dp", None),
            P("ep", None, "dp", None),
        ),
        check_vma=False,
    )
```

profile of v0, /device:TPU:97, one launch (start us, length us, event | category | flops | bytes accessed | tf_op | source)
XLA Modules:
  0.0 671.3 jit_solution(20847825409527018)
XLA Ops:
  11.1 4.3 scatter_custom_fusion.2
  15.7 8.0 %gather_fusion = bf16[1280]{0:T(1024)(128)(2,1)S(1)} fusion(bf16[1024]{0:T(1024)(128)(2,1)S(1)} %reshape.292, s32[2048]{0:T(1024)S(1)} %pad_clamp_fusion.1), kind=kCustom, calls=%fused_computation.5 | custom fusion | bytes 10240 | tf_op jit(solution)/shard_map/jit(_take)/gather | solution.py:166
  24.5 16.8 %all-to-all-start = ((bf16[128,10,1]{1,2,0:T(2,128)(2,1)}), bf16[128,10,1]{1,2,0:T(2,128)(2,1)S(1)}, u32[]{:S(2)}, u32[]{:S(2)}) async-start(bf16[128,10,1]{1,2,0:T(2,128)(2,1)} %all_to_all.119), calls=%async_computation | async-start | bytes 131072 | tf_op jit(solution)/shard_map/all_to_all | solution.py:171
  42.0 3.1 reduce.13
  47.3 13.0 %all-to-all-start.7 = ((bf16[128,2,768]{2,1,0:T(2,128)(2,1)}), bf16[128,2,768]{2,1,0:T(2,128)(2,1)S(1)}, u32[]{:S(2)}, u32[]{:S(2)}) async-start(bf16[128,2,768]{2,1,0:T(2,128)(2,1)} %reshape.424), calls=%async_computation.7 | async-start | bytes 786432 | tf_op jit(solution)/shard_map/all_to_all | solution.py:91
  60.4 3.1 reduce.14
  64.4 8.8 %all-to-all-done.7 = bf16[128,2,768]{2,1,0:T(2,128)(2,1)S(1)} async-done(((bf16[128,2,768]{2,1,0:T(2,128)(2,1)}), bf16[128,2,768]{2,1,0:T(2,128)(2,1)S(1)}, u32[]{:S(2)}, u32[]{:S(2)}) %all-to-all-start.7) | async-done | bytes 393248 | tf_op jit(solution)/shard_map/all_to_all | solution.py:91
  73.2 11.0 %all-to-all-start.9 = ((bf16[128,2,768]{2,1,0:T(2,128)(2,1)}), bf16[128,2,768]{2,1,0:T(2,128)(2,1)S(1)}, u32[]{:S(2)}, u32[]{:S(2)}) async-start(bf16[128,2,768]{2,1,0:T(2,128)(2,1)} %reshape.428), calls=%async_computation.10 | async-start | bytes 786432 | tf_op jit(solution)/shard_map/all_to_all | solution.py:92
  86.6 3.1 reduce.15
  90.6 6.7 all-to-all-done.9
  97.2 11.0 %all-to-all-start.11 = ((bf16[128,2,768]{2,1,0:T(2,128)(2,1)}), bf16[128,2,768]{2,1,0:T(2,128)(2,1)S(1)}, u32[]{:S(2)}, u32[]{:S(2)}) async-start(bf16[128,2,768]{2,1,0:T(2,128)(2,1)} %reshape.432), calls=%async_computation.12 | async-start | bytes 786432 | tf_op jit(solution)/shard_map/all_to_all | solution.py:93
  109.9 11.4 %all-to-all-done.11 = bf16[128,2,768]{2,1,0:T(2,128)(2,1)S(1)} async-done(((bf16[128,2,768]{2,1,0:T(2,128)(2,1)}), bf16[128,2,768]{2,1,0:T(2,128)(2,1)S(1)}, u32[]{:S(2)}, u32[]{:S(2)}) %all-to-all-start.11) | async-done | bytes 393248 | tf_op jit(solution)/shard_map/all_to_all | solution.py:93
  121.3 11.2 %all-to-all-start.2 = ((f32[128,1,1536]{2,1,0:T(1,128)}), f32[128,1,1536]{2,1,0:T(1,128)S(1)}, u32[]{:S(2)}, u32[]{:S(2)}) async-start(f32[128,1,1536]{2,1,0:T(1,128)} %all_to_all.92), calls=%async_computation.2 | async-start | bytes 1572864 | tf_op jit(solution)/shard_map/all_to_all | solution.py:78
  140.7 13.4 %all-to-all-done.2 = f32[128,1,1536]{2,1,0:T(1,128)S(1)} async-done(((f32[128,1,1536]{2,1,0:T(1,128)}), f32[128,1,1536]{2,1,0:T(1,128)S(1)}, u32[]{:S(2)}, u32[]{:S(2)}) %all-to-all-start.2) | async-done | bytes 786464 | tf_op jit(solution)/shard_map/all_to_all | solution.py:78
  154.1 10.5 %all-to-all-start.8 = ((bf16[128,2,768]{2,1,0:T(2,128)(2,1)}), bf16[128,2,768]{2,1,0:T(2,128)(2,1)S(1)}, u32[]{:S(2)}, u32[]{:S(2)}) async-start(bf16[128,2,768]{2,1,0:T(2,128)(2,1)} %reshape.426), calls=%async_computation.8 | async-start | bytes 786432 | tf_op jit(solution)/shard_map/all_to_all | solution.py:99
  167.3 10.3 %all-to-all-done.8 = bf16[128,2,768]{2,1,0:T(2,128)(2,1)S(1)} async-done(((bf16[128,2,768]{2,1,0:T(2,128)(2,1)}), bf16[128,2,768]{2,1,0:T(2,128)(2,1)S(1)}, u32[]{:S(2)}, u32[]{:S(2)}) %all-to-all-start.8) | async-done | bytes 393248 | tf_op jit(solution)/shard_map/all_to_all | solution.py:99
  177.7 12.0 %all-to-all-start.3 = ((f32[128,1,1536]{2,1,0:T(1,128)}), f32[128,1,1536]{2,1,0:T(1,128)}, u32[]{:S(2)}, u32[]{:S(2)}) async-start(f32[128,1,1536]{2,1,0:T(1,128)} %copy.47), calls=%async_computation.3 | async-start | bytes 1572864 | tf_op jit(solution)/shard_map/all_to_all | solution.py:80
  189.7 5.1 gather_fusion.5
  194.8 5.1 gather_fusion.4
  199.9 4.2 select_select_fusion
  204.1 6.0 all_to_all.96
  211.0 13.3 %all-to-all-start.4 = ((bf16[128,10,1024]{2,1,0:T(8,128)(2,1)}), bf16[128,10,1024]{2,1,0:T(8,128)(2,1)}, u32[]{:S(2)}, u32[]{:S(2)}) async-start(bf16[128,10,1024]{2,1,0:T(8,128)(2,1)} %all_to_all.96), calls=%async_computation.4 | async-start | bytes 8388608 | tf_op jit(solution)/shard_map/all_to_all | solution.py:169
  227.1 100.1 %all-to-all-done.4 = bf16[128,10,1024]{2,1,0:T(8,128)(2,1)} async-done(((bf16[128,10,1024]{2,1,0:T(8,128)(2,1)}), bf16[128,10,1024]{2,1,0:T(8,128)(2,1)}, u32[]{:S(2)}, u32[]{:S(2)}) %all-to-all-start.4) | async-done | bytes 2621472 | tf_op jit(solution)/shard_map/all_to_all | solution.py:169
  327.1 10.5 %all-to-all-start.1 = ((bf16[128,10,1024]{2,1,0:T(8,128)(2,1)}), bf16[128,10,1024]{2,1,0:T(8,128)(2,1)}, u32[]{:S(2)}, u32[]{:S(2)}) async-start(bf16[128,10,1024]{2,1,0:T(8,128)(2,1)} %all_to_all.90), calls=%async_computation.1 | async-start | bytes 8388608 | tf_op jit(solution)/shard_map/all_to_all | solution.py:170
  337.6 3.0 reduce.1
  345.3 95.1 %all-to-all-done.1 = bf16[128,10,1024]{2,1,0:T(8,128)(2,1)} async-done(((bf16[128,10,1024]{2,1,0:T(8,128)(2,1)}), bf16[128,10,1024]{2,1,0:T(8,128)(2,1)}, u32[]{:S(2)}, u32[]{:S(2)}) %all-to-all-start.1) | async-done | bytes 2621472 | tf_op jit(solution)/shard_map/all_to_all | solution.py:170
  440.4 10.0 %all-to-all-start.10 = ((bf16[128,2,768]{2,1,0:T(2,128)(2,1)}), bf16[128,2,768]{2,1,0:T(2,128)(2,1)S(1)}, u32[]{:S(2)}, u32[]{:S(2)}) async-start(bf16[128,2,768]{2,1,0:T(2,128)(2,1)} %reshape.430), calls=%async_computation.11 | async-start | bytes 786432 | tf_op jit(solution)/shard_map/all_to_all | solution.py:100
  450.4 4.9 multiply_convert_fusion
  455.3 6.1 convert_element_type.149
  461.4 6.7 reshape.295
  468.1 5.9 copy.48
  474.0 6.1 all_to_all.98
  480.2 4.9 fusion.13
  485.1 13.7 %all-to-all-start.12 = ((bf16[128,2,768]{2,1,0:T(2,128)(2,1)}), bf16[128,2,768]{2,1,0:T(2,128)(2,1)S(1)}, u32[]{:S(2)}, u32[]{:S(2)}) async-start(bf16[128,2,768]{2,1,0:T(2,128)(2,1)} %reshape.434), calls=%async_computation.13 | async-start | bytes 786432 | tf_op jit(solution)/shard_map/all_to_all | solution.py:101
  498.8 4.7 multiply_reduce_fusion
  504.3 5.3 fusion.2
  511.9 11.4 %all-to-all-start.6 = ((bf16[128,10,1]{1,2,0:T(2,128)(2,1)}), bf16[128,10,1]{1,2,0:T(2,128)(2,1)S(1)}, u32[]{:S(2)}, u32[]{:S(2)}) async-start(bf16[128,10,1]{1,2,0:T(2,128)(2,1)} %convert_element_type.171), calls=%async_computation.6 | async-start | bytes 131072 | tf_op jit(solution)/shard_map/all_to_all | solution.py:187
  523.3 4.2 convolution_convert_fusion
  527.5 6.0 all_to_all.99
  533.5 14.3 %all-to-all-start.5 = ((bf16[128,10,1024]{2,1,0:T(8,128)(2,1)}), bf16[128,10,1024]{2,1,0:T(8,128)(2,1)}, u32[]{:S(2)}, u32[]{:S(2)}) async-start(bf16[128,10,1024]{2,1,0:T(8,128)(2,1)} %all_to_all.99), calls=%async_computation.5 | async-start | bytes 8388608 | tf_op jit(solution)/shard_map/all_to_all | solution.py:186
  548.3 3.4 fusion.8
  551.7 4.2 fusion.7
  573.5 6.8 %gather_fusion.3 = bf16[1024]{0:T(1024)(128)(2,1)S(1)} fusion(bf16[1280]{0:T(1024)(128)(2,1)S(1)} %all_to_all.103, s32[1024]{0:T(1024)S(1)} %broadcast_clamp_fusion), kind=kCustom, calls=%fused_computation.8 | custom fusion | bytes 8192 | tf_op jit(solution)/shard_map/jit(_take)/gather | solution.py:198
  581.1 6.8 %reduce-scatter.2.cloned.1.call-done = bf16[1,2,256,384]{3,2,1,0:T(8,128)(2,1)} async-done(((bf16[1,2,1024,384]{3,2,1,0:T(8,128)(2,1)}), bf16[1,2,256,384]{3,2,1,0:T(8,128)(2,1)}) %reduce-scatter.2.cloned.1.call-update) | async-done | bytes 393232 | tf_op jit(solution)/shard_map/reduce_scatter | solution.py:190
  590.8 59.8 %all-to-all-done.5 = bf16[128,10,1024]{2,1,0:T(8,128)(2,1)} async-done(((bf16[128,10,1024]{2,1,0:T(8,128)(2,1)}), bf16[128,10,1024]{2,1,0:T(8,128)(2,1)}, u32[]{:S(2)}, u32[]{:S(2)}) %all-to-all-start.5) | async-done | bytes 2621472 | tf_op jit(solution)/shard_map/all_to_all | solution.py:186
  650.7 4.8 all_to_all.101
  655.5 5.3 gather_fusion.2
  660.8 3.4 fusion.5
  (127 shorter events, 57.6 us)
Async XLA Ops:
  7.2 182.5 %copy-start = (bf16[128,1024]{1,0:T(8,128)(2,1)S(1)}, bf16[128,1024]{1,0:T(8,128)(2,1)}, u32[]{:S(2)}) copy-start(bf16[128,1024]{1,0:T(8,128)(2,1)} %param.13) | copy-start | bytes 786436
  7.2 8.3 %copy-start.17 = (bf16[128,8]{0,1:T(8,128)(2,1)S(1)}, bf16[128,8]{0,1:T(8,128)(2,1)}, u32[]{:S(2)}) copy-start(bf16[128,8]{0,1:T(8,128)(2,1)} %param.15) | copy-start | bytes 6148
  11.1 30.2 %copy-start.15 = (bf16[1,2,256,384]{3,2,1,0:T(8,128)(2,1)S(1)}, bf16[1,2,256,384]{3,2,1,0:T(8,128)(2,1)}, u32[]{:S(2)}) copy-start(bf16[1,2,256,384]{3,2,1,0:T(8,128)(2,1)} %param.19) | copy-start | bytes 1179652
  23.7 36.6 %copy-start.16 = (bf16[1,2,256,384]{3,2,1,0:T(8,128)(2,1)S(1)}, bf16[1,2,256,384]{3,2,1,0:T(8,128)(2,1)}, u32[]{:S(2)}) copy-start(bf16[1,2,256,384]{3,2,1,0:T(8,128)(2,1)} %param.20) | copy-start | bytes 1179652
  24.5 22.8 %all-to-all-start = ((bf16[128,10,1]{1,2,0:T(2,128)(2,1)}), bf16[128,10,1]{1,2,0:T(2,128)(2,1)S(1)}, u32[]{:S(2)}, u32[]{:S(2)}) async-start(bf16[128,10,1]{1,2,0:T(2,128)(2,1)} %all_to_all.119), calls=%async_computation | async-start | bytes 131072 | tf_op jit(solution)/shard_map/all_to_all | solution.py:171
  47.3 25.9 %all-to-all-start.7 = ((bf16[128,2,768]{2,1,0:T(2,128)(2,1)}), bf16[128,2,768]{2,1,0:T(2,128)(2,1)S(1)}, u32[]{:S(2)}, u32[]{:S(2)}) async-start(bf16[128,2,768]{2,1,0:T(2,128)(2,1)} %reshape.424), calls=%async_computation.7 | async-start | bytes 786432 | tf_op jit(solution)/shard_map/all_to_all | solution.py:91
  63.5 44.7 %copy-start.14 = (f32[1,2,256,384]{3,2,1,0:T(8,128)S(1)}, f32[1,2,256,384]{3,2,1,0:T(8,128)}, u32[]{:S(2)}) copy-start(f32[1,2,256,384]{3,2,1,0:T(8,128)} %param.18) | copy-start | bytes 2359300
  73.2 24.1 %all-to-all-start.9 = ((bf16[128,2,768]{2,1,0:T(2,128)(2,1)}), bf16[128,2,768]{2,1,0:T(2,128)(2,1)S(1)}, u32[]{:S(2)}, u32[]{:S(2)}) async-start(bf16[128,2,768]{2,1,0:T(2,128)(2,1)} %reshape.428), calls=%async_computation.10 | async-start | bytes 786432 | tf_op jit(solution)/shard_map/all_to_all | solution.py:92
  97.2 24.1 %all-to-all-start.11 = ((bf16[128,2,768]{2,1,0:T(2,128)(2,1)}), bf16[128,2,768]{2,1,0:T(2,128)(2,1)S(1)}, u32[]{:S(2)}, u32[]{:S(2)}) async-start(bf16[128,2,768]{2,1,0:T(2,128)(2,1)} %reshape.432), calls=%async_computation.12 | async-start | bytes 786432 | tf_op jit(solution)/shard_map/all_to_all | solution.py:93
  121.3 11.2 %copy-start.10 = (bf16[128,2,768]{2,1,0:T(2,128)(2,1)}, bf16[128,2,768]{2,1,0:T(2,128)(2,1)S(1)}, u32[]{:S(2)}) copy-start(bf16[128,2,768]{2,1,0:T(2,128)(2,1)S(1)} %all-to-all-done.11) | copy-start | bytes 1179652
  121.3 32.8 %all-to-all-start.2 = ((f32[128,1,1536]{2,1,0:T(1,128)}), f32[128,1,1536]{2,1,0:T(1,128)S(1)}, u32[]{:S(2)}, u32[]{:S(2)}) async-start(f32[128,1,1536]{2,1,0:T(1,128)} %all_to_all.92), calls=%async_computation.2 | async-start | bytes 1572864 | tf_op jit(solution)/shard_map/all_to_all | solution.py:78
  135.0 1.6 copy-start.11
  137.0 1.0 copy-start.12
  137.0 1.1 copy-start.13
  154.1 23.5 %all-to-all-start.8 = ((bf16[128,2,768]{2,1,0:T(2,128)(2,1)}), bf16[128,2,768]{2,1,0:T(2,128)(2,1)S(1)}, u32[]{:S(2)}, u32[]{:S(2)}) async-start(bf16[128,2,768]{2,1,0:T(2,128)(2,1)} %reshape.426), calls=%async_computation.8 | async-start | bytes 786432 | tf_op jit(solution)/shard_map/all_to_all | solution.py:99
  177.7 17.1 %copy-start.6 = (bf16[128,2,768]{2,1,0:T(2,128)(2,1)}, bf16[128,2,768]{2,1,0:T(2,128)(2,1)S(1)}, u32[]{:S(2)}) copy-start(bf16[128,2,768]{2,1,0:T(2,128)(2,1)S(1)} %all-to-all-done.8) | copy-start | bytes 1179652
  177.7 33.3 %all-to-all-start.3 = ((f32[128,1,1536]{2,1,0:T(1,128)}), f32[128,1,1536]{2,1,0:T(1,128)}, u32[]{:S(2)}, u32[]{:S(2)}) async-start(f32[128,1,1536]{2,1,0:T(1,128)} %copy.47), calls=%async_computation.3 | async-start | bytes 1572864 | tf_op jit(solution)/shard_map/all_to_all | solution.py:80
  189.7 5.1 copy-start.2
  211.0 116.1 %all-to-all-start.4 = ((bf16[128,10,1024]{2,1,0:T(8,128)(2,1)}), bf16[128,10,1024]{2,1,0:T(8,128)(2,1)}, u32[]{:S(2)}, u32[]{:S(2)}) async-start(bf16[128,10,1024]{2,1,0:T(8,128)(2,1)} %all_to_all.96), calls=%async_computation.4 | async-start | bytes 8388608 | tf_op jit(solution)/shard_map/all_to_all | solution.py:169
  327.1 113.3 %all-to-all-start.1 = ((bf16[128,10,1024]{2,1,0:T(8,128)(2,1)}), bf16[128,10,1024]{2,1,0:T(8,128)(2,1)}, u32[]{:S(2)}, u32[]{:S(2)}) async-start(bf16[128,10,1024]{2,1,0:T(8,128)(2,1)} %all_to_all.90), calls=%async_computation.1 | async-start | bytes 8388608 | tf_op jit(solution)/shard_map/all_to_all | solution.py:170
  337.6 4.2 copy-start.5
  337.6 142.6 %all-gather.2.cloned.1.call-start = ((), (), s32[]{:S(2)}) async-start(), calls=%async_computation.14 | async-start | bytes 1966080 | tf_op jit(solution)/shard_map/all_gather | solution.py:152
  440.4 44.7 %all-to-all-start.10 = ((bf16[128,2,768]{2,1,0:T(2,128)(2,1)}), bf16[128,2,768]{2,1,0:T(2,128)(2,1)S(1)}, u32[]{:S(2)}, u32[]{:S(2)}) async-start(bf16[128,2,768]{2,1,0:T(2,128)(2,1)} %reshape.430), calls=%async_computation.11 | async-start | bytes 786432 | tf_op jit(solution)/shard_map/all_to_all | solution.py:100
  480.2 18.6 %copy-start.18 = (bf16[1,2,1024,384]{3,2,1,0:T(8,128)(2,1)S(1)}, bf16[1,2,1024,384]{3,2,1,0:T(8,128)(2,1)}, u32[]{:S(2)}) copy-start(bf16[1,2,1024,384]{3,2,1,0:T(8,128)(2,1)} %all-gather.2.cloned.1.call-done) | copy-start | bytes 4718596
  485.1 18.5 %copy-start.8 = (bf16[128,2,768]{2,1,0:T(2,128)(2,1)}, bf16[128,2,768]{2,1,0:T(2,128)(2,1)S(1)}, u32[]{:S(2)}) copy-start(bf16[128,2,768]{2,1,0:T(2,128)(2,1)S(1)} %all-to-all-done.10) | copy-start | bytes 1179652
  485.1 26.8 %all-to-all-start.12 = ((bf16[128,2,768]{2,1,0:T(2,128)(2,1)}), bf16[128,2,768]{2,1,0:T(2,128)(2,1)S(1)}, u32[]{:S(2)}, u32[]{:S(2)}) async-start(bf16[128,2,768]{2,1,0:T(2,128)(2,1)} %reshape.434), calls=%async_computation.13 | async-start | bytes 786432 | tf_op jit(solution)/shard_map/all_to_all | solution.py:101
  511.9 21.6 %copy-start.9 = (bf16[128,2,768]{2,1,0:T(2,128)(2,1)}, bf16[128,2,768]{2,1,0:T(2,128)(2,1)S(1)}, u32[]{:S(2)}) copy-start(bf16[128,2,768]{2,1,0:T(2,128)(2,1)S(1)} %all-to-all-done.12) | copy-start | bytes 1179652
  511.9 21.6 %all-to-all-start.6 = ((bf16[128,10,1]{1,2,0:T(2,128)(2,1)}), bf16[128,10,1]{1,2,0:T(2,128)(2,1)S(1)}, u32[]{:S(2)}, u32[]{:S(2)}) async-start(bf16[128,10,1]{1,2,0:T(2,128)(2,1)} %convert_element_type.171), calls=%async_computation.6 | async-start | bytes 131072 | tf_op jit(solution)/shard_map/all_to_all | solution.py:187
  533.5 14.7 %copy-start.19 = (bf16[1280,384]{1,0:T(8,128)(2,1)S(1)}, bf16[1280,384]{1,0:T(8,128)(2,1)}, u32[]{:S(2)}) copy-start(bf16[1280,384]{1,0:T(8,128)(2,1)} %fusion.2) | copy-start | bytes 2949124
  533.5 117.1 %all-to-all-start.5 = ((bf16[128,10,1024]{2,1,0:T(8,128)(2,1)}), bf16[128,10,1024]{2,1,0:T(8,128)(2,1)}, u32[]{:S(2)}, u32[]{:S(2)}) async-start(bf16[128,10,1024]{2,1,0:T(8,128)(2,1)} %all_to_all.99), calls=%async_computation.5 | async-start | bytes 8388608 | tf_op jit(solution)/shard_map/all_to_all | solution.py:186
  547.9 40.1 %reduce-scatter.2.cloned.1.call-start = ((), (), s32[]{:S(2)}) async-start(), calls=%async_computation.15 | async-start | bytes 1966080 | tf_op jit(solution)/shard_map/reduce_scatter | solution.py:190
  548.2 3.5 copy-start.20
  555.9 1.5 copy-start.7
  572.1 15.9 %copy-start.3 = (f32[1,2,256,384]{3,2,1,0:T(8,128)S(1)}, f32[1,2,256,384]{3,2,1,0:T(8,128)}, u32[]{:S(2)}) copy-start(f32[1,2,256,384]{3,2,1,0:T(8,128)} %mul.138) | copy-start | bytes 2359300
  573.2 14.8 %copy-start.4 = (f32[1,2,256,384]{3,2,1,0:T(8,128)S(1)}, f32[1,2,256,384]{3,2,1,0:T(8,128)}, u32[]{:S(2)}) copy-start(f32[1,2,256,384]{3,2,1,0:T(8,128)} %mul.144) | copy-start | bytes 2359300
  655.5 8.8 %copy-start.1 = (bf16[128,1024]{1,0:T(8,128)(2,1)S(1)}, bf16[128,1024]{1,0:T(8,128)(2,1)}, u32[]{:S(2)}) copy-start(bf16[128,1024]{1,0:T(8,128)(2,1)} %param.13) | copy-start | bytes 786436
Sparse Core Ops, SparseCore 0:
  341.8 32.3 all-gather.1
  557.4 30.5 reduce-scatter.1
where the time goes:
time: 681 us; the launch traced here: 671 us
  waiting for transfers between devices  317 us (47%)
  starting transfers between devices  159 us (23%)
  local copies, waits for them, and re-layouts  111 us (16%)
  other arithmetic  42.6 us (6%)
  matrix products  27.3 us (4%)
  between operations  15 us (2%)
    all_to_all x1, waiting for transfers between devices, shards(): lax.all_to_all(send_rows, 'ep', split_axis=0, concat_axis=0, tiled=True)  100 us
    all_to_all x1, waiting for transfers between devices, shards(): lax.all_to_all(send_cotan, 'ep', split_axis=0, concat_axis=0, tiled=True)  95.1 us
    all_to_all x1, waiting for transfers between devices, shards(): lax.all_to_all(pair_grad, 'ep', split_axis=0, concat_axis=0, tiled=True)  59.8 us
    all_to_all x1, starting transfers between devices, shards(): lax.all_to_all(send_weight, 'ep', split_axis=0, concat_axis=0, tiled=True)  16.8 us
    all_to_all x1, starting transfers between devices, shards(): lax.all_to_all(pair_grad, 'ep', split_axis=0, concat_axis=0, tiled=True)  14.3 us
    unnamed x61, local copies, waits for them, and re-layouts  14 us
    all_to_all x1, starting transfers between devices, relocate_moments(): lax.all_to_all(average_arranged, 'ep', split_axis=0, concat_axis=0, tiled...  13.7 us
  transfers between devices with their start and end apart: 15, of which 12 were waited for; matrix products, arithmetic and copies ran while one was open for 19% of the time, Pallas kernels for 0%

commit v1 on v0

v1 whole, which is shorter than its diff:
```python
import functools
import jax
import jax.numpy as jnp
from jax import lax
from jax.experimental import pallas as pl
from jax.experimental.pallas import tpu as pltpu
from jax.sharding import PartitionSpec as P

LEARN_RATE = 0.01
BETA_ONE = 0.9
BETA_TWO = 0.95
ADAM_EPS = 1e-08
EMA_DECAY = 0.99

MESH = pl.DeviceIdType.MESH
BF = jnp.bfloat16
F32 = jnp.float32
RING = 8
PEERS = 16
CAP = 10
BLOCK = RING * CAP
SLOTS = PEERS * BLOCK
TOK = 128
HALF = TOK // 2
D = 1024
FF = 384
LANES_A = 640
LANES_B = 512


def place():
    me = lax.axis_index("ep")
    dp = lax.axis_index("dp")
    y = me // PEERS
    z = lax.rem(me, PEERS) // 2
    core = lax.rem(me, 2)
    return dp, y, z, core


def row_device(dp, y, z, core):
    def device(q):
        return (y * PEERS + q, dp)

    return device


def col_device(dp, y, z, core):
    def device(q):
        return ((q // 2) * PEERS + z * 2 + lax.rem(q, 2), dp)

    return device


def greet(row_of, col_of, row_mine, col_mine):
    barrier = pltpu.get_barrier_semaphore()

    def signal(step, carry):
        for device_of, mine in ((row_of, row_mine), (col_of, col_mine)):
            pl.semaphore_signal(
                barrier,
                inc=1,
                device_id=device_of(lax.rem(mine + step, PEERS)),
                device_id_type=MESH,
            )
        return carry

    lax.fori_loop(1, PEERS, signal, 0)
    pl.semaphore_wait(barrier, 2 * (PEERS - 1))


def one_hot_block(code_row, values):
    slot = lax.broadcasted_iota(jnp.int32, (BLOCK, RING * TOK), 0).astype(F32)
    return jnp.where(code_row == slot, values, 0.0).astype(BF)


def send_kernel(
    xa_ref, cb_ref, xr_ref, sr_ref, code_a, code_b,
    xall, call, gate, xs, cs, ag_send, ag_recv, a2a_send, a2a_recv, local,
):
    dp, y, z, core = place()
    row_of, col_of = row_device(dp, y, z, core), col_device(dp, y, z, core)
    row_mine, col_mine = z * 2 + core, y * 2 + core
    greet(row_of, col_of, row_mine, col_mine)

    rings = (
        (xa_ref, xall, y, lambda v: (v * PEERS + z * 2 + core, dp)),
        (cb_ref, call, z, lambda v: (y * PEERS + v * 2 + core, dp)),
    )

    def piece(ring, way, step, half):
        own, everyone, at, device = rings[ring]
        sign = 1 if way == 0 else RING - 1
        source = lax.rem(at + (RING - sign) * step, RING)
        rows = pl.ds(half * HALF, HALF)
        src = own.at[rows] if step == 0 else everyone.at[source, rows]
        return pltpu.make_async_remote_copy(
            src_ref=src,
            dst_ref=everyone.at[source, rows],
            send_sem=ag_send.at[ring, way, step, half],
            recv_sem=ag_recv.at[ring, way, step, half],
            device_id=device(lax.rem(at + sign, RING)),
            device_id_type=MESH,
        )

    def arrival(ring, way, step, half):
        own, everyone, at, device = rings[ring]
        sign = 1 if way == 0 else RING - 1
        source = lax.rem(at + (RING - sign) * (step + 1), RING)
        rows = pl.ds(half * HALF, HALF)
        return pltpu.make_async_remote_copy(
            src_ref=own.at[rows],
            dst_ref=everyone.at[source, rows],
            send_sem=ag_send.at[ring, way, step, half],
            recv_sem=ag_recv.at[ring, way, step, half],
            device_id=device(lax.rem(at + sign, RING)),
            device_id_type=MESH,
        )

    def sent(step, way, half):
        return step < 3 or way == half

    for step in range(4):
        for half in range(2):
            for ring in range(2):
                for way in range(2):
                    if step > 0:
                        arrival(ring, way, step - 1, half).wait_recv()
                    if sent(step, way, half):
                        piece(ring, way, step, half).start()
        if step == 0:
            for ring in range(2):
                own, everyone, at, device = rings[ring]
                everyone[at] = own[...]
    for ring in range(2):
        for way in range(2):
            arrival(ring, way, 3, way).wait_recv()

    for source in range(RING):
        lanes = pl.ds(source * TOK, TOK)
        rows_a = pl.ds(pl.multiple_of(y * PEERS, PEERS), PEERS)
        rows_b = pl.ds(pl.multiple_of(z * PEERS, PEERS), PEERS)
        rank_a = xall[source, rows_a, D : D + TOK].astype(F32)
        rank_b = call[source, rows_b, D : D + TOK].astype(F32)
        code_a[:, lanes] = jnp.where(rank_a < 0, -1.0, rank_a + source * CAP)
        code_b[:, lanes] = jnp.where(rank_b < 0, -1.0, rank_b + source * CAP)
        gate[:, lanes] = call[source, rows_b, D + TOK :].astype(F32)

    def exchange(path, slot_here, slot_there, peer):
        src, dst, device = ((xs, xr_ref, row_of), (cs, sr_ref, col_of))[path]
        return pltpu.make_async_remote_copy(
            src_ref=src.at[slot_here],
            dst_ref=dst.at[slot_there],
            send_sem=a2a_send.at[path, slot_here],
            recv_sem=a2a_recv.at[path, slot_there],
            device_id=device(peer),
            device_id_type=MESH,
        )

    group = 4

    def build(step, carry):
        for path in range(2):
            mine = (row_mine, col_mine)[path]
            first = lax.rem(mine // group + step, PEERS // group) * group
            hots = []
            for k in range(group):
                line = pl.ds(first + k, 1)
                if path == 0:
                    hots.append(one_hot_block(code_a[line, :], 1.0))
                else:
                    hots.append(one_hot_block(code_b[line, :], gate[line, :]))
            hot = jnp.concatenate(hots, axis=0)
            source = (xall, call)[path]
            table = source[:, :, :D].reshape(RING * TOK, D)
            rows = jnp.dot(hot, table, preferred_element_type=F32).astype(BF)
            buffer = (xs, cs)[path]
            for k in range(group):
                buffer[first + k] = rows[k * BLOCK : (k + 1) * BLOCK]
            for k in range(group):
                peer = first + k

                @pl.when(peer != mine)
                def _():
                    exchange(path, peer, mine, peer).start()

        return carry

    lax.fori_loop(0, PEERS // group, build, 0)
    own_a = pltpu.make_async_copy(xs.at[row_mine], xr_ref.at[row_mine], local.at[0])
    own_b = pltpu.make_async_copy(cs.at[col_mine], sr_ref.at[col_mine], local.at[1])
    own_a.start()
    own_b.start()

    def finish(step, carry):
        for path in range(2):
            mine = (row_mine, col_mine)[path]
            peer = lax.rem(mine + step, PEERS)
            exchange(path, peer, mine, peer).wait_send()
            exchange(path, mine, peer, peer).wait_recv()
        return carry

    lax.fori_loop(1, PEERS, finish, 0)
    own_a.wait()
    own_b.wait()
    for step in range(4):
        for half in range(2):
            for ring in range(2):
                for way in range(2):
                    if sent(step, way, half):
                        piece(ring, way, step, half).wait_send()


def send(xa, cb):
    vm = pl.BlockSpec(memory_space=pltpu.VMEM)
    return pl.pallas_call(
        send_kernel,
        out_shape=[
            jax.ShapeDtypeStruct((PEERS, BLOCK, D), BF),
            jax.ShapeDtypeStruct((PEERS, BLOCK, D), BF),
            jax.ShapeDtypeStruct((PEERS, RING * TOK), F32),
            jax.ShapeDtypeStruct((PEERS, RING * TOK), F32),
        ],
        in_specs=[vm] * 2,
        out_specs=[vm] * 4,
        scratch_shapes=[
            pltpu.VMEM((RING, TOK, xa.shape[1]), BF),
            pltpu.VMEM((RING, TOK, cb.shape[1]), BF),
            pltpu.VMEM((PEERS, RING * TOK), F32),
            pltpu.VMEM((PEERS, BLOCK, D), BF),
            pltpu.VMEM((PEERS, BLOCK, D), BF),
            pltpu.SemaphoreType.DMA((2, 2, 4, 2)),
            pltpu.SemaphoreType.DMA((2, 2, 4, 2)),
            pltpu.SemaphoreType.DMA((2, PEERS)),
            pltpu.SemaphoreType.DMA((2, PEERS)),
            pltpu.SemaphoreType.DMA((2,)),
        ],
        compiler_params=pltpu.CompilerParams(
            collective_id=0, has_side_effects=True, vmem_limit_bytes=56 * 2**20
        ),
        name="send_rows",
    )(xa, cb)


def swap_block(which):
    shape = (BLOCK, SLOTS)
    row = lax.broadcasted_iota(jnp.int32, shape, 0)
    lane = lax.broadcasted_iota(jnp.int32, shape, 1)
    outer = sum(((row >= CAP * k).astype(jnp.int32) for k in range(1, RING)))
    rank = row - outer * CAP
    target = (outer * 2 + lax.rem(which, 2)) * BLOCK + (which // 2) * CAP + rank
    return jnp.where(lane == target, 1.0, 0.0).astype(BF)


def expert_kernel(
    xr_ref, sr_ref, w_ref, pay_a, pay_b, ag_ref, hid_b_ref, hg_hi, hg_lo, hid
):
    me = lax.axis_index("ep")
    group = 4
    rows_per = group * BLOCK
    up = w_ref.at[0]
    down = w_ref.at[1]

    def first(step, carry):
        rows = pl.ds(pl.multiple_of(step * rows_per, rows_per), rows_per)
        hg = jnp.dot(sr_ref[rows, :], down[...], preferred_element_type=F32)
        hi = hg.astype(BF)
        hg_hi[rows, :] = hi
        hg_lo[rows, :] = (hg - hi.astype(F32)).astype(BF)
        return carry

    lax.fori_loop(0, PEERS // group, first, 0)

    def second(step, carry):
        rows = pl.ds(pl.multiple_of(step * rows_per, rows_per), rows_per)
        swap = jnp.concatenate([swap_block(step * group + k) for k in range(group)], axis=0)
        hg = jnp.dot(swap, hg_hi[...], preferred_element_type=F32) + jnp.dot(
            swap, hg_lo[...], preferred_element_type=F32
        )
        act = jnp.dot(xr_ref[rows, :], up[...], preferred_element_type=F32)
        sigma = jax.nn.sigmoid(act)
        hidden = (act * sigma).astype(BF)
        act_grad = (hg * sigma * (1.0 + act * (1.0 - sigma))).astype(BF)
        gate = jnp.sum(hg * hidden.astype(F32), axis=1, keepdims=True)
        hid[rows, :] = hidden
        ag_ref[rows, :] = act_grad
        pair = lax.dot_general(
            act_grad, up[: LANES_A - TOK, :], (((1,), (1,)), ((), ())), preferred_element_type=F32
        )
        lane = lax.broadcasted_iota(jnp.int32, (rows_per, TOK), 1)
        pay_a[rows, : LANES_A - TOK] = pair.astype(BF)
        pay_a[rows, LANES_A - TOK :] = jnp.where(lane == me, gate, 0.0).astype(BF)
        return carry

    lax.fori_loop(0, PEERS // group, second, 0)

    def third(step, carry):
        rows = pl.ds(pl.multiple_of(step * rows_per, rows_per), rows_per)
        swap = jnp.concatenate([swap_block(step * group + k) for k in range(group)], axis=0)
        act_grad = jnp.dot(swap, ag_ref[...], preferred_element_type=F32).astype(BF)
        hid_b_ref[rows, :] = jnp.dot(swap, hid[...], preferred_element_type=F32).astype(BF)
        pair = lax.dot_general(
            act_grad, up[LANES_A - TOK :, :], (((1,), (1,)), ((), ())), preferred_element_type=F32
        )
        pay_b[rows, :] = pair.astype(BF)
        return carry

    lax.fori_loop(0, PEERS // group, third, 0)


def expert(xr, sr, weights):
    vm = pl.BlockSpec(memory_space=pltpu.VMEM)
    return pl.pallas_call(
        expert_kernel,
        out_shape=[
            jax.ShapeDtypeStruct((SLOTS, LANES_A), BF),
            jax.ShapeDtypeStruct((SLOTS, LANES_B), BF),
            jax.ShapeDtypeStruct((SLOTS, FF), BF),
            jax.ShapeDtypeStruct((SLOTS, FF), BF),
        ],
        in_specs=[vm] * 3,
        out_specs=[vm] * 4,
        scratch_shapes=[pltpu.VMEM((SLOTS, FF), BF)] * 3,
        compiler_params=pltpu.CompilerParams(vmem_limit_bytes=56 * 2**20),
        name="expert",
    )(xr, sr, weights)


def return_kernel(
    pay_a, pay_b, code_a, code_b, out_a, out_b,
    back_a, back_b, part_a, part_b, run_a, run_b, got_a, got_b,
    a2a_send, a2a_recv, rs_send, rs_recv, local,
):
    dp, y, z, core = place()
    row_of, col_of = row_device(dp, y, z, core), col_device(dp, y, z, core)
    row_mine, col_mine = z * 2 + core, y * 2 + core
    greet(row_of, col_of, row_mine, col_mine)

    def exchange(path, slot_here, slot_there, peer):
        src, dst, device = ((pay_a, back_a, row_of), (pay_b, back_b, col_of))[path]
        return pltpu.make_async_remote_copy(
            src_ref=src.at[slot_here],
            dst_ref=dst.at[slot_there],
            send_sem=a2a_send.at[path, slot_here],
            recv_sem=a2a_recv.at[path, slot_there],
            device_id=device(peer),
            device_id_type=MESH,
        )

    def begin(step, carry):
        for path in range(2):
            mine = (row_mine, col_mine)[path]
            peer = lax.rem(mine + step, PEERS)
            exchange(path, peer, mine, peer).start()
        return carry

    lax.fori_loop(1, PEERS, begin, 0)
    own_a = pltpu.make_async_copy(pay_a.at[row_mine], back_a.at[row_mine], local.at[0])
    own_b = pltpu.make_async_copy(pay_b.at[col_mine], back_b.at[col_mine], local.at[1])
    own_a.start()
    own_b.start()

    def finish(step, carry):
        for path in range(2):
            mine = (row_mine, col_mine)[path]
            peer = lax.rem(mine + step, PEERS)
            exchange(path, peer, mine, peer).wait_send()
            exchange(path, mine, peer, peer).wait_recv()
        return carry

    lax.fori_loop(1, PEERS, finish, 0)
    own_a.wait()
    own_b.wait()

    def combine(path, owner):
        code = (code_a, code_b)[path]
        back = (back_a, back_b)[path]
        lanes = pl.ds(pl.multiple_of(owner * TOK, TOK), TOK)
        slot = lax.broadcasted_iota(jnp.int32, (BLOCK, TOK), 0).astype(F32)
        hot = jnp.concatenate(
            [
                jnp.where(code[k : k + 1, lanes] == slot, 1.0, 0.0).astype(BF)
                for k in range(PEERS)
            ],
            axis=0,
        )
        width = (LANES_A, LANES_B)[path]
        return lax.dot_general(
            hot, back[...].reshape(SLOTS, width), (((0,), (0,)), ((), ())),
            preferred_element_type=F32,
        )

    def sums(owner, carry):
        part_a[owner] = combine(0, owner).astype(BF)
        part_b[owner] = combine(1, owner).astype(BF)
        return carry

    lax.fori_loop(0, RING, sums, 0)

    rings = (
        (part_a, run_a, got_a, y, lambda v: (v * PEERS + z * 2 + core, dp)),
        (part_b, run_b, got_b, z, lambda v: (y * PEERS + v * 2 + core, dp)),
    )

    def halves(way, step):
        return (way,) if step == 0 else (0, 1)

    def hop(ring, way, step, half):
        part, run, got, at, device = rings[ring]
        sign = 1 if way == 0 else RING - 1
        rows = pl.ds(half * HALF, HALF)
        return pltpu.make_async_remote_copy(
            src_ref=run.at[way, step, rows],
            dst_ref=got.at[way, step, rows],
            send_sem=rs_send.at[ring, way, step, half],
            recv_sem=rs_recv.at[ring, way, step, half],
            device_id=device(lax.rem(at + sign, RING)),
            device_id_type=MESH,
        )

    for step in range(4):
        for half in range(2):
            for ring in range(2):
                part, run, got, at, device = rings[ring]
                rows = pl.ds(half * HALF, HALF)
                for way in range(2):
                    if half not in halves(way, step):
                        continue
                    sign = 1 if way == 0 else RING - 1
                    owner = lax.rem(at + sign * (4 - step), RING)
                    total = part[owner, rows]
                    if step > 0 and half in halves(way, step - 1):
                        hop(ring, way, step - 1, half).wait_recv()
                        total = (total.astype(F32) + got[way, step - 1, rows].astype(F32)).astype(BF)
                    run[way, step, rows] = total
                    hop(ring, way, step, half).start()
    for half in range(2):
        for ring in range(2):
            part, run, got, at, device = rings[ring]
            rows = pl.ds(half * HALF, HALF)
            total = part[at, rows].astype(F32)
            for way in range(2):
                hop(ring, way, 3, half).wait_recv()
                total = total + got[way, 3, rows].astype(F32)
            (out_a, out_b)[ring][rows] = total.astype(BF)
    for step in range(4):
        for ring in range(2):
            for way in range(2):
                for half in halves(way, step):
                    hop(ring, way, step, half).wait_send()


def give_back(pay_a, pay_b, code_a, code_b):
    vm = pl.BlockSpec(memory_space=pltpu.VMEM)
    widths = (LANES_A, LANES_B)
    return pl.pallas_call(
        return_kernel,
        out_shape=[jax.ShapeDtypeStruct((TOK, w), BF) for w in widths],
        in_specs=[vm] * 4,
        out_specs=[vm] * 2,
        scratch_shapes=[pltpu.VMEM((PEERS, BLOCK, w), BF) for w in widths]
        + [pltpu.VMEM((RING, TOK, w), BF) for w in widths]
        + [pltpu.VMEM((2, 4, TOK, w), BF) for w in widths]
        + [pltpu.VMEM((2, 4, TOK, w), BF) for w in widths]
        + [
            pltpu.SemaphoreType.DMA((2, PEERS)),
            pltpu.SemaphoreType.DMA((2, PEERS)),
            pltpu.SemaphoreType.DMA((2, 2, 4, 2)),
            pltpu.SemaphoreType.DMA((2, 2, 4, 2)),
            pltpu.SemaphoreType.DMA((2,)),
        ],
        compiler_params=pltpu.CompilerParams(
            collective_id=1, has_side_effects=True, vmem_limit_bytes=56 * 2**20
        ),
        name="return_rows",
    )(pay_a.reshape(PEERS, BLOCK, LANES_A), pay_b.reshape(PEERS, BLOCK, LANES_B), code_a, code_b)


def moved(plan, index):
    gone = index[..., None]
    step = jnp.where(gone == plan[:, 0], plan[:, 1] - gone, 0) + jnp.where(
        gone == plan[:, 1], plan[:, 0] - gone, 0
    )
    return index + jnp.sum(step, axis=-1)


def adam_update(master, moment_one, moment_two, average, gradient):
    first = BETA_ONE * moment_one.astype(F32) + (1.0 - BETA_ONE) * gradient
    second = BETA_TWO * moment_two.astype(F32) + (1.0 - BETA_TWO) * gradient * gradient
    fresh = master - LEARN_RATE * first / (jnp.sqrt(second) + ADAM_EPS)
    smooth = EMA_DECAY * average.astype(F32) + (1.0 - EMA_DECAY) * fresh
    return (fresh, first.astype(BF), second.astype(BF), smooth.astype(BF))


def relocate(state, holder):
    pieces = lax.all_to_all(state, "ep", split_axis=0, concat_axis=0, tiled=True)
    arranged = jnp.take(pieces, holder, axis=0)
    return lax.all_to_all(arranged, "ep", split_axis=0, concat_axis=0, tiled=True)


def shards(
    tokens, expert_ids, gate_weights, cotangent, migration_plan,
    master, moment_one, moment_two, average,
):
    count = lax.axis_size("ep")
    me = lax.axis_index("ep")
    holder = moved(migration_plan, jnp.arange(count, dtype=jnp.int32))
    target = moved(migration_plan, expert_ids)

    shape = master.shape
    state = jnp.concatenate(
        [v.astype(BF).reshape(-1, FF) for v in (master, moment_one, moment_two, average)], axis=0
    ).reshape(count, -1, FF)
    state = relocate(state, holder).reshape(4, *shape)
    weights, moment_one, moment_two, average = state[0], state[1], state[2], state[3]
    stays = jnp.sum((migration_plan == me).astype(jnp.int32)) == 0
    master = jnp.where(stays, master, weights.astype(F32))
    gathered = lax.all_gather(weights[0], "dp", axis=1, tiled=True)

    columns = jnp.arange(count, dtype=jnp.int32)
    hits = columns[:, None, None] == target.T[None]
    chosen = jnp.any(hits, axis=1)
    gates = jnp.sum(jnp.where(hits, gate_weights.T[None], 0), axis=1).astype(BF)
    before = (jnp.arange(TOK)[:, None] < jnp.arange(TOK)[None, :]).astype(BF)
    rank = jnp.dot(chosen.astype(BF), before, preferred_element_type=F32)
    rank = jnp.where(chosen, rank, -1.0).astype(BF)

    def by_column(table):
        return table.reshape(RING, RING, 2, TOK).transpose(1, 0, 2, 3).reshape(count, TOK)

    xa = jnp.concatenate([tokens, rank], axis=1)
    cb = jnp.concatenate([cotangent, by_column(rank), by_column(gates)], axis=1)
    xr, sr, code_a, code_b = send(xa, cb)
    xr = xr.reshape(SLOTS, D)
    sr = sr.reshape(SLOTS, D)
    pay_a, pay_b, act_grad, hidden = expert(xr, sr, gathered)
    over_rows = (((0,), (0,)), ((), ()))
    up_grad = lax.dot_general(xr, act_grad, over_rows, preferred_element_type=F32)
    down_grad = lax.dot_general(sr, hidden, over_rows, preferred_element_type=F32)
    grad = jnp.stack([up_grad, down_grad]).astype(BF)
    grad = lax.psum_scatter(grad, "dp", scatter_dimension=1, tiled=True).astype(F32)[None]
    sum_a, sum_b = give_back(pay_a, pay_b, code_a, code_b)
    new_master, first, second, smooth = adam_update(master, moment_one, moment_two, average, grad)
    token_grad = jnp.concatenate([sum_a[:, : LANES_A - TOK], sum_b], axis=1)
    gate_sums = sum_a[:, LANES_A - TOK :].astype(F32)
    picked = jnp.sum(
        jnp.where(target[:, :, None] == columns[None, None, :], gate_sums[:, None, :], 0.0), axis=2
    )
    gate_grad = (picked / gate_weights.astype(F32)).astype(BF)
    return (token_grad, gate_grad, new_master, first, second, smooth)


def solution(mesh):
    rows = P(("ep", "dp"), None)
    held = P("ep", None, "dp", None)
    return jax.shard_map(
        shards,
        mesh=mesh,
        in_specs=(rows, rows, rows, rows, P(), held, held, held, held),
        out_specs=(rows, rows, held, held, held, held),
        check_vma=False,
    )
```

time: 681 us -> 334 us (0.49)
  the two profiles are of different devices: /device:TPU:97 before, /device:TPU:1 now
where the time goes in v1:
time: 334 us; the launch traced here: 333 us
  Pallas kernels  185 us (55%)
  blocking collectives  48.7 us (15%)
  waiting for transfers between devices  41 us (12%)
  starting transfers between devices  18.8 us (6%)
  other arithmetic  15.8 us (5%)
  between operations  14.9 us (4%)
  matrix products  4.6 us (1%)
  local copies, waits for them, and re-layouts  4.22 us (1%)
    pallas_call x1, Pallas kernels, send(): pl.pallas_call(send_kernel, out_shape=[jax.ShapeDtypeStruct((PEERS, BLOCK...  94 us
    pallas_call x1, Pallas kernels, give_back(): pl.pallas_call(return_kernel, out_shape=[jax.ShapeDtypeStruct((TOK, w), B...  73 us
    all_to_all x1, blocking collectives, relocate(): lax.all_to_all(arranged, 'ep', split_axis=0, concat_axis=0, tiled=True)  48.7 us
    all_to_all x1, waiting for transfers between devices, relocate(): lax.all_to_all(state, 'ep', split_axis=0, concat_axis=0, tiled=True)  40.9 us
    all_to_all x1, starting transfers between devices, relocate(): lax.all_to_all(state, 'ep', split_axis=0, concat_axis=0, tiled=True)  18.6 us
    pallas_call x1, Pallas kernels, expert(): pl.pallas_call(expert_kernel, out_shape=[jax.ShapeDtypeStruct((SLOTS, LAN...  18.3 us
  transfers between devices with their start and end apart: 3, of which 1 were waited for; matrix products, arithmetic and copies ran while one was open for 3% of the time, Pallas kernels for 50%

profile of v1, /device:TPU:1, one launch (start us, length us, event | category | flops | bytes accessed | tf_op | source)
XLA Modules:
  0.0 333.4 jit_solution(10961587384728700465)
XLA Ops:
  7.2 1.2 convert_element_type.80
  8.3 2.5 pad_maximum_fusion
  10.9 18.6 %all-to-all-start = ((bf16[128,16,384]{2,1,0:T(8,128)(2,1)}), bf16[128,16,384]{2,1,0:T(8,128)(2,1)S(1)}, u32[]{:S(2)}, u32[]{:S(2)}) async-start(bf16[128,16,384]{2,1,0:T(8,128)(2,1)} %bitcast.16), calls=%async_computation | async-start | bytes 3145728 | tf_op jit(solution)/shard_map/all_to_all | solution.py:495
  29.5 0.0 all-gather.2.cloned.1.call-start
  29.5 0.0 copy-done.10
  29.5 0.1 add_reduce_fusion.1
  29.6 40.9 %all-to-all-done = bf16[128,16,384]{2,1,0:T(8,128)(2,1)S(1)} async-done(((bf16[128,16,384]{2,1,0:T(8,128)(2,1)}), bf16[128,16,384]{2,1,0:T(8,128)(2,1)S(1)}, u32[]{:S(2)}, u32[]{:S(2)}) %all-to-all-start) | async-done | bytes 1572896 | tf_op jit(solution)/shard_map/all_to_all | solution.py:495
  70.6 0.9 gather_fusion
  71.5 0.3 broadcast_select_fusion
  71.7 0.0 copy-start.8
  71.7 0.0 copy-start.9
  71.7 0.0 copy-start.6
  71.8 48.7 %all_to_all.10 = bf16[128,16,384]{2,1,0:T(8,128)(2,1)S(1)} all-to-all(bf16[128,16,384]{2,1,0:T(8,128)(2,1)S(1)} %broadcast_select_fusion), channel_id=1, replica_groups=mesh['ep'=128,'dp'=4] {'ep'}, dimensions={0} | all-to-all | bytes 3145728 | tf_op jit(solution)/shard_map/all_to_all | solution.py:497
  120.4 0.8 slice.44
  121.2 0.0 all-gather.2.cloned.1.call-update
  121.2 0.2 reduce-scatter.2.cloned.1.call-start
  121.5 0.0 copy-done.8
  121.5 0.1 add_reduce_fusion
  121.6 0.2 fusion.7
  121.8 0.1 fusion.2
  121.9 0.0 copy-done.9
  121.9 0.2 fusion.12
  122.2 0.7 pad_maximum_fusion.3.xa_ref
  122.9 0.0 copy-done.7
  122.9 0.7 pad_maximum_fusion.2.cb_ref
  123.7 94.0 %send_rows.1 = (bf16[16,80,1024]{2,1,0:T(8,128)(2,1)}, bf16[16,80,1024]{2,1,0:T(8,128)(2,1)}, f32[16,1024]{1,0:T(8,128)}, f32[16,1024]{1,0:T(8,128)}) custom-call(bf16[128,1152]{1,0:T(8,128)(2,1)} %pad_maximum_fusion.3.xa_ref, bf16[128,1280]{1,0:T(8,128)(2,1)} %pad_maximum_fusion.2.cb_ref), custom_call_target="tpu_custom_call" | custom-call | tf_op jit(solution)/shard_map/send_rows/pallas_call | solution.py:215
  217.7 0.0 all-gather.2.cloned.1.call-done.w_ref
  217.7 18.3 %expert.1 = (bf16[1280,640]{1,0:T(8,128)(2,1)}, bf16[1280,512]{1,0:T(8,128)(2,1)}, bf16[1280,384]{1,0:T(8,128)(2,1)}, bf16[1280,384]{1,0:T(8,128)(2,1)}) custom-call(bf16[1280,1024]{1,0:T(8,128)(2,1)} %bitcast.77, bf16[1280,1024]{1,0:T(8,128)(2,1)} %bitcast.75, bf16[2,1024,384]{2,1,0:T(8,128)(2,1)} %all-gather.2.cloned.1.call-done.w_ref), custom_call_target="tpu_custom_call" | custom-call | tf_op jit(solution)/shard_map/expert/pallas_call | solution.py:312
  236.1 2.9 fusion
  239.0 0.0 copy-done.3
  239.0 0.0 copy-done.11
  239.0 1.6 fusion.1
  240.6 1.3 pad_maximum_fusion.1
  241.9 0.0 reduce-scatter.2.cloned.1.call-update
  241.9 0.1 copy.24
  242.0 0.1 copy.25
  242.1 0.6 fusion.13
  243.4 1.1 convert_multiply_fusion.3
  244.5 73.0 %return_rows.1 = (bf16[128,640]{1,0:T(8,128)(2,1)}, bf16[128,512]{1,0:T(8,128)(2,1)}) custom-call(bf16[16,80,640]{2,1,0:T(8,128)(2,1)} %bitcast.79, bf16[16,80,512]{2,1,0:T(8,128)(2,1)} %bitcast.81, f32[16,1024]{1,0:T(8,128)} %get-tuple-element.20.code_a, f32[16,1024]{1,0:T(8,128)} %get-tuple-element.21.code_b), custom_call_target="tpu_custom_call" | custom-call | tf_op jit(solution)/shard_map/return_rows/pallas_call | solution.py:455
  317.6 1.6 slice.37
  319.2 0.8 slice_convert_fusion
  319.9 0.4 select_reduce_fusion
  320.3 0.7 copy.26
  321.0 1.8 pad_maximum_fusion.4
  322.8 2.1 fusion.10
  324.9 0.0 copy-done.1
  325.0 0.0 copy-done.5
  325.0 1.6 add_convert_fusion
  (22 shorter events, 0.1 us)
Async XLA Ops:
  10.9 18.6 %copy-start.10 = (s32[8,2]{0,1:T(2,128)S(1)}, s32[8,2]{0,1:T(2,128)}, u32[]{:S(2)}) copy-start(s32[8,2]{0,1:T(2,128)} %param.13) | copy-start | bytes 196
  10.9 59.7 %all-to-all-start = ((bf16[128,16,384]{2,1,0:T(8,128)(2,1)}), bf16[128,16,384]{2,1,0:T(8,128)(2,1)S(1)}, u32[]{:S(2)}, u32[]{:S(2)}) async-start(bf16[128,16,384]{2,1,0:T(8,128)(2,1)} %bitcast.16), calls=%async_computation | async-start | bytes 3145728 | tf_op jit(solution)/shard_map/all_to_all | solution.py:495
  29.5 188.3 %all-gather.2.cloned.1.call-start = ((), (), s32[]{:S(2)}) async-start(), calls=%async_computation.3 | async-start | bytes 1966080 | tf_op jit(solution)/shard_map/all_gather | solution.py:517
  71.7 49.7 %copy-start.8 = (s32[128,8]{0,1:T(8,128)S(1)}, s32[128,8]{0,1:T(8,128)}, u32[]{:S(2)}) copy-start(s32[128,8]{0,1:T(8,128)} %param.10) | copy-start | bytes 12292
  71.7 50.2 %copy-start.9 = (bf16[128,8]{0,1:T(8,128)(2,1)S(1)}, bf16[128,8]{0,1:T(8,128)(2,1)}, u32[]{:S(2)}) copy-start(bf16[128,8]{0,1:T(8,128)(2,1)} %param.11) | copy-start | bytes 6148
  71.7 50.4 %copy-start.6 = (bf16[128,1024]{1,0:T(8,128)(2,1)S(1)}, bf16[128,1024]{1,0:T(8,128)(2,1)}, u32[]{:S(2)}) copy-start(bf16[128,1024]{1,0:T(8,128)(2,1)} %param.9) | copy-start | bytes 786436
  120.4 2.5 copy-start.7
  121.2 201.6 %reduce-scatter.2.cloned.1.call-start = ((), (), s32[]{:S(2)}) async-start(), calls=%async_computation.4 | async-start | bytes 1966080 | tf_op jit(solution)/shard_map/reduce_scatter | solution.py:540
  217.7 18.3 %copy-start.4 = (bf16[16,80,1024]{2,1,0:T(8,128)(2,1)S(1)}, bf16[16,80,1024]{2,1,0:T(8,128)(2,1)}, u32[]{:S(2)}) copy-start(bf16[16,80,1024]{2,1,0:T(8,128)(2,1)} %get-tuple-element.16) | copy-start | bytes 7864324
  236.1 2.9 copy-start.3
  236.1 2.9 copy-start.11
  321.0 4.0 %copy-start = (bf16[32,16,384]{2,1,0:T(8,128)(2,1)S(1)}, bf16[32,16,384]{2,1,0:T(8,128)(2,1)}, u32[]{:S(2)}) copy-start(bf16[32,16,384]{2,1,0:T(8,128)(2,1)} %slice.44) | copy-start | bytes 1179652
  321.0 4.0 %copy-start.1 = (f32[32,16,384]{2,1,0:T(8,128)S(1)}, f32[32,16,384]{2,1,0:T(8,128)}, u32[]{:S(2)}) copy-start(f32[32,16,384]{2,1,0:T(8,128)} %get-tuple-element.35) | copy-start | bytes 2359300
  321.0 4.0 %copy-start.2 = (f32[1,2,256,384]{3,2,1,0:T(8,128)S(1)}, f32[1,2,256,384]{3,2,1,0:T(8,128)}, u32[]{:S(2)}) copy-start(f32[1,2,256,384]{3,2,1,0:T(8,128)} %param.14) | copy-start | bytes 2359300
  322.8 2.2 copy-start.5
Sparse Core Ops, SparseCore 0:
  121.4 26.5 all-gather.1
  242.0 30.2 reduce-scatter.1

commit v2 on v1

v2 whole, which is shorter than its diff:
```python
import functools
import jax
import jax.numpy as jnp
from jax import lax
from jax.experimental import pallas as pl
from jax.experimental.pallas import tpu as pltpu
from jax.sharding import PartitionSpec as P

LEARN_RATE = 0.01
BETA_ONE = 0.9
BETA_TWO = 0.95
ADAM_EPS = 1e-08
EMA_DECAY = 0.99

MESH = pl.DeviceIdType.MESH
BF = jnp.bfloat16
F32 = jnp.float32
RING = 8
PEERS = 16
CAP = 10
BLOCK = RING * CAP
SLOTS = PEERS * BLOCK
TOK = 128
HALF = TOK // 2
D = 1024
FF = 384
LANES_A = 640
LANES_B = 512


def place():
    me = lax.axis_index("ep")
    dp = lax.axis_index("dp")
    y = me // PEERS
    z = lax.rem(me, PEERS) // 2
    core = lax.rem(me, 2)
    return dp, y, z, core


def row_device(dp, y, z, core):
    def device(q):
        return (y * PEERS + q, dp)

    return device


def col_device(dp, y, z, core):
    def device(q):
        return ((q // 2) * PEERS + z * 2 + lax.rem(q, 2), dp)

    return device


def one_hot_block(code_row, values):
    slot = lax.broadcasted_iota(jnp.int32, (BLOCK, RING * TOK), 0).astype(F32)
    return jnp.where(code_row == slot, values, 0.0).astype(BF)


def swap_block(which):
    shape = (BLOCK, SLOTS)
    row = lax.broadcasted_iota(jnp.int32, shape, 0)
    lane = lax.broadcasted_iota(jnp.int32, shape, 1)
    outer = sum(((row >= CAP * k).astype(jnp.int32) for k in range(1, RING)))
    rank = row - outer * CAP
    target = (outer * 2 + lax.rem(which, 2)) * BLOCK + (which // 2) * CAP + rank
    return jnp.where(lane == target, 1.0, 0.0).astype(BF)


def layer_kernel(
    xa_ref, cb_ref, state, perm,
    out_a, out_b, grad_ref, fin_r, fin_c,
    xall, call, code_a, code_b, gate, xs, cs, xr, sr,
    s1, s2, arr, g1,
    wts, hg_hi, hg_lo, act_ref, hid, ag, hid_b,
    pay_a, pay_b, back_a, back_b, part_a, part_b,
    run_a, run_b, got_a, got_b, grads, grad_run, grad_got,
    ag_send, ag_recv, out_send, out_recv, home_send, home_recv, rs_send, rs_recv,
    mig_send, mig_recv, mig_local, wt_send, wt_recv, gr_send, gr_recv, local,
):
    dp, y, z, core = place()
    me = lax.axis_index("ep")
    n_dp = lax.axis_size("dp")
    row_of, col_of = row_device(dp, y, z, core), col_device(dp, y, z, core)
    row_mine, col_mine = z * 2 + core, y * 2 + core
    x_right, x_left = lax.rem(dp + 1, n_dp), lax.rem(dp + 3, n_dp)
    x_far = lax.rem(dp + 2, n_dp)
    mines = (row_mine, col_mine)

    barrier = pltpu.get_barrier_semaphore()

    def signal(step, carry):
        for device_of, mine in ((row_of, row_mine), (col_of, col_mine)):
            pl.semaphore_signal(
                barrier, inc=1,
                device_id=device_of(lax.rem(mine + step, PEERS)), device_id_type=MESH,
            )
        return carry

    lax.fori_loop(1, PEERS, signal, 0)
    for other in (x_right, x_left):
        pl.semaphore_signal(barrier, inc=1, device_id=(me, other), device_id_type=MESH)
    pl.semaphore_wait(barrier, 2 * (PEERS - 1) + 2)

    rings = (
        (xa_ref, xall, y, lambda v: (v * PEERS + z * 2 + core, dp)),
        (cb_ref, call, z, lambda v: (y * PEERS + v * 2 + core, dp)),
    )

    def piece(ring, way, step, half, arriving=False):
        own, everyone, at, device = rings[ring]
        sign = 1 if way == 0 else RING - 1
        back = step + 1 if arriving else step
        source = lax.rem(at + (RING - sign) * back, RING)
        rows = pl.ds(half * HALF, HALF)
        src = own.at[rows] if step == 0 or arriving else everyone.at[source, rows]
        return pltpu.make_async_remote_copy(
            src_ref=src,
            dst_ref=everyone.at[source, rows],
            send_sem=ag_send.at[ring, way, step, half],
            recv_sem=ag_recv.at[ring, way, step, half],
            device_id=device(lax.rem(at + sign, RING)),
            device_id_type=MESH,
        )

    def sent(step, way, half):
        return step < 3 or way == half

    firsts, seconds = (z, y), (y, z)

    def mig_plan(which, stage):
        if stage in (0, 3):
            to = (
                (lambda s: (y * PEERS + s, dp)) if which == 0
                else (lambda s: ((s // 2) * PEERS + z * 2 + lax.rem(s, 2), dp))
            )
        else:
            to = (
                (lambda v: (v * PEERS + z * 2 + core, dp)) if which == 0
                else (lambda v: (y * PEERS + v * 2 + core, dp))
            )
        if stage == 0:
            src = (lambda u: state.at[0, :, u]) if which == 0 else (lambda u: state.at[1, u])
            return (lambda u: to(u * 2 + which)), src, (lambda s: s1.at[s])
        if stage == 1:
            return to, (lambda v: s1.at[:, v]), (lambda v: s2.at[pl.ds(v * PEERS, PEERS)])
        if stage == 2:
            return to, (lambda v: arr.at[pl.ds(v * PEERS, PEERS)]), (lambda v: g1.at[v])
        dst = (lambda u: fin_r.at[:, u]) if which == 0 else (lambda u: fin_c.at[u])
        return to, (lambda s: g1.at[:, s]), dst

    def migrate(which, stage, peer, place_there):
        to, src, dst = mig_plan(which, stage)
        return pltpu.make_async_remote_copy(
            src_ref=src(peer),
            dst_ref=dst(place_there),
            send_sem=mig_send.at[which, stage, peer],
            recv_sem=mig_recv.at[which, stage, place_there],
            device_id=to(peer),
            device_id_type=MESH,
        )

    def mig_own(which, stage):
        _, src, dst = mig_plan(which, stage)
        here = (
            (firsts[which], mines[which]),
            (seconds[which], seconds[which]),
            (seconds[which], seconds[which]),
            (mines[which], firsts[which]),
        )[stage]
        return pltpu.make_async_copy(src(here[0]), dst(here[1]), mig_local.at[which, stage])

    def mig_sends(which, stage, act):
        if stage == 0:
            first = firsts[which]

            def go(step, carry):
                act(lax.rem(first + step, RING), mines[which])
                return carry

            lax.fori_loop(1, RING, go, 0)

            @pl.when(core != which)
            def _():
                act(first, mines[which])
        else:
            count, at, slot = (
                (PEERS, mines[which], firsts[which]) if stage == 3
                else (RING, seconds[which], seconds[which])
            )

            @pl.when(core == which)
            def _():
                def go(step, carry):
                    act(lax.rem(at + step, count), slot)
                    return carry

                lax.fori_loop(1, count, go, 0)

    def mig_start(stage):
        for which in range(2):
            mig_sends(which, stage, lambda peer, slot: migrate(which, stage, peer, slot).start())

            @pl.when(core == which)
            def _():
                mig_own(which, stage).start()

    def mig_wait(stage):
        for which in range(2):
            mig_sends(which, stage, lambda peer, slot: migrate(which, stage, peer, slot).wait_send())
            if stage == 3:
                first = firsts[which]

                def hold(step, carry):
                    migrate(which, stage, mines[which], lax.rem(first + step, RING)).wait_recv()
                    return carry

                lax.fori_loop(1, RING, hold, 0)

                @pl.when(core != which)
                def _():
                    migrate(which, stage, mines[which], first).wait_recv()

                @pl.when(core == which)
                def _():
                    mig_own(which, stage).wait()
            else:
                count, at = (PEERS, mines[which]) if stage == 0 else (RING, seconds[which])

                @pl.when(core == which)
                def _():
                    def hold(step, carry):
                        slot = lax.rem(at + step, count)
                        peer = firsts[which] if stage == 0 else slot
                        migrate(which, stage, peer, slot).wait_recv()
                        return carry

                    lax.fori_loop(1, count, hold, 0)
                    mig_own(which, stage).wait()

    for step in range(4):
        for half in range(2):
            for ring in range(2):
                for way in range(2):
                    if step > 0:
                        piece(ring, way, step - 1, half, True).wait_recv()
                    if sent(step, way, half):
                        piece(ring, way, step, half).start()
        if step == 0:
            mig_start(0)
            for ring in range(2):
                own, everyone, at, device = rings[ring]
                everyone[at] = own[...]
    for ring in range(2):
        for way in range(2):
            piece(ring, way, 3, way, True).wait_recv()

    for source in range(RING):
        lanes = pl.ds(source * TOK, TOK)
        rows_a = pl.ds(pl.multiple_of(y * PEERS, PEERS), PEERS)
        rows_b = pl.ds(pl.multiple_of(z * PEERS, PEERS), PEERS)
        rank_a = xall[source, rows_a, D : D + TOK].astype(F32)
        rank_b = call[source, rows_b, D : D + TOK].astype(F32)
        code_a[:, lanes] = jnp.where(rank_a < 0, -1.0, rank_a + source * CAP)
        code_b[:, lanes] = jnp.where(rank_b < 0, -1.0, rank_b + source * CAP)
        gate[:, lanes] = call[source, rows_b, D + TOK :].astype(F32)

    def exchange(path, slot_here, slot_there, peer):
        src, dst, device = ((xs, xr, row_of), (cs, sr, col_of))[path]
        return pltpu.make_async_remote_copy(
            src_ref=src.at[slot_here],
            dst_ref=dst.at[slot_there],
            send_sem=out_send.at[path, slot_here],
            recv_sem=out_recv.at[path, slot_there],
            device_id=device(peer),
            device_id_type=MESH,
        )

    group = 4
    n_group = PEERS // group
    rows_per = group * BLOCK

    def build(path, step):
        mine = mines[path]
        first = lax.rem(mine // group + step, n_group) * group
        hots = []
        for k in range(group):
            line = pl.ds(first + k, 1)
            if path == 0:
                hots.append(one_hot_block(code_a[line, :], 1.0))
            else:
                hots.append(one_hot_block(code_b[line, :], gate[line, :]))
        hot = jnp.concatenate(hots, axis=0)
        source = (xall, call)[path]
        table = source[:, :, :D].reshape(RING * TOK, D)
        rows = jnp.dot(hot, table, preferred_element_type=F32).astype(BF)
        buffer = (xs, cs)[path]
        buffer[pl.ds(first, group)] = rows.reshape(group, BLOCK, D)
        for k in range(group):
            peer = first + k

            @pl.when(peer != mine)
            def _():
                exchange(path, peer, mine, peer).start()

    def weight_piece(way, step, half, arriving=False):
        back = step + 1 if arriving else step
        sign = 1 if way == 0 else 3
        source = lax.rem(dp + (4 - sign) * back, n_dp)
        part = wts.at[half, source]
        return pltpu.make_async_remote_copy(
            src_ref=part,
            dst_ref=part,
            send_sem=wt_send.at[way, step, half],
            recv_sem=wt_recv.at[way, step, half],
            device_id=(me, lax.rem(dp + sign, n_dp)),
            device_id_type=MESH,
        )

    def reorder(p, carry):
        arr[p] = s2[perm[core, p]]
        return carry

    for step in range(n_group):
        build(0, step)
        build(1, step)
        mig_wait(step)
        if step == 1:
            lax.fori_loop(0, PEERS * RING, reorder, 0)
        if step < 3:
            mig_start(step + 1)
    for half in range(2):
        wts[half, dp] = fin_r[half * 2 : half * 2 + 2].reshape(D // 4, FF)
        for way in range(2):
            weight_piece(way, 0, half).start()
    own_a = pltpu.make_async_copy(xs.at[row_mine], xr.at[row_mine], local.at[0])
    own_b = pltpu.make_async_copy(cs.at[col_mine], sr.at[col_mine], local.at[1])
    own_a.start()
    own_b.start()
    for way in range(2):
        weight_piece(way, 0, way, True).wait_recv()
        weight_piece(way, 1, way).start()
    for way in range(2):
        weight_piece(way, 0, 1 - way, True).wait_recv()
        weight_piece(way, 1, way, True).wait_recv()
    own_a.wait()
    own_b.wait()

    up = wts.at[0]
    down = wts.at[1]

    def rows_of(ref, first):
        block = ref[pl.ds(first, group)]
        return block.reshape(rows_per, block.shape[-1])

    def flat(first):
        return pl.ds(pl.multiple_of(first * BLOCK, rows_per), rows_per)

    def project(step, carry):
        for path in range(2):
            mine = mines[path]
            first = lax.rem(mine // group + n_group - step, n_group) * group
            for k in range(group):
                peer = first + k

                @pl.when(peer != mine)
                def _():
                    exchange(path, mine, peer, peer).wait_recv()

            if path == 0:
                act_ref[flat(first), :] = jnp.dot(
                    rows_of(xr, first), up[...].reshape(D, FF), preferred_element_type=F32
                )
            else:
                hg = jnp.dot(
                    rows_of(sr, first), down[...].reshape(D, FF), preferred_element_type=F32
                )
                hi = hg.astype(BF)
                hg_hi[flat(first), :] = hi
                hg_lo[flat(first), :] = (hg - hi.astype(F32)).astype(BF)
        return carry

    lax.fori_loop(0, n_group, project, 0)

    def home(path, slot_here, slot_there, peer):
        src, dst, device = ((pay_a, back_a, row_of), (pay_b, back_b, col_of))[path]
        return pltpu.make_async_remote_copy(
            src_ref=src.at[slot_here],
            dst_ref=dst.at[slot_there],
            send_sem=home_send.at[path, slot_here],
            recv_sem=home_recv.at[path, slot_there],
            device_id=device(peer),
            device_id_type=MESH,
        )

    def send_home(path, first):
        for k in range(group):
            peer = first + k

            @pl.when(peer != mines[path])
            def _():
                home(path, peer, mines[path], peer).start()

    def swaps(first):
        return jnp.concatenate([swap_block(first + k) for k in range(group)], axis=0)

    width_a = LANES_A - TOK

    def backward(step, carry):
        first = lax.rem(row_mine // group + step, n_group) * group
        rows = flat(first)
        swap = swaps(first)
        hg = jnp.dot(swap, hg_hi[...], preferred_element_type=F32) + jnp.dot(
            swap, hg_lo[...], preferred_element_type=F32
        )
        act = act_ref[rows, :]
        sigma = jax.nn.sigmoid(act)
        hidden = (act * sigma).astype(BF)
        act_grad = (hg * sigma * (1.0 + act * (1.0 - sigma))).astype(BF)
        gates = jnp.sum(hg * hidden.astype(F32), axis=1, keepdims=True)
        hid[rows, :] = hidden
        ag[rows, :] = act_grad
        pair = lax.dot_general(
            act_grad, up[0:2].reshape(width_a, FF), (((1,), (1,)), ((), ())),
            preferred_element_type=F32,
        )
        lane = lax.broadcasted_iota(jnp.int32, (rows_per, TOK), 1)
        here = pl.ds(first, group)
        pay_a[here, :, :width_a] = pair.astype(BF).reshape(group, BLOCK, width_a)
        pay_a[here, :, width_a:] = (
            jnp.where(lane == me, gates, 0.0).astype(BF).reshape(group, BLOCK, TOK)
        )
        send_home(0, first)
        return carry

    lax.fori_loop(0, n_group, backward, 0)

    def swapped(step, carry):
        first = lax.rem(col_mine // group + step, n_group) * group
        rows = flat(first)
        swap = swaps(first)
        act_grad = jnp.dot(swap, ag[...], preferred_element_type=F32).astype(BF)
        hid_b[rows, :] = jnp.dot(swap, hid[...], preferred_element_type=F32).astype(BF)
        pair = lax.dot_general(
            act_grad, up[2:4].reshape(LANES_B, FF), (((1,), (1,)), ((), ())),
            preferred_element_type=F32,
        )
        pay_b[pl.ds(first, group)] = pair.astype(BF).reshape(group, BLOCK, LANES_B)
        send_home(1, first)
        return carry

    lax.fori_loop(0, n_group, swapped, 0)
    own_a = pltpu.make_async_copy(pay_a.at[row_mine], back_a.at[row_mine], local.at[0])
    own_b = pltpu.make_async_copy(pay_b.at[col_mine], back_b.at[col_mine], local.at[1])
    own_a.start()
    own_b.start()

    over_rows = (((0,), (0,)), ((), ()))

    def weight_grads(step, carry):
        lanes = pl.ds(pl.multiple_of(step * 256, 256), 256)
        grads[0, step] = lax.dot_general(
            xr[:, :, lanes].reshape(SLOTS, 256), ag[...], over_rows, preferred_element_type=F32
        ).astype(BF)
        grads[1, step] = lax.dot_general(
            sr[:, :, lanes].reshape(SLOTS, 256), hid_b[...], over_rows, preferred_element_type=F32
        ).astype(BF)
        return carry

    lax.fori_loop(0, n_dp, weight_grads, 0)

    def grad_hop(way, step, half):
        return pltpu.make_async_remote_copy(
            src_ref=grads.at[half, x_far] if step == 0 else grad_run.at[way, half],
            dst_ref=grad_got.at[way, step, half],
            send_sem=gr_send.at[way, step, half],
            recv_sem=gr_recv.at[way, step, half],
            device_id=(me, (x_right, x_left)[way]),
            device_id_type=MESH,
        )

    for way in range(2):
        grad_hop(way, 0, way).start()
    for way in range(2):
        owner = (x_right, x_left)[way]
        for half in (1 - way, way):
            total = grads[half, owner]
            if half == way:
                grad_hop(way, 0, way).wait_recv()
                total = (total.astype(F32) + grad_got[way, 0, half].astype(F32)).astype(BF)
            grad_run[way, half] = total
            grad_hop(way, 1, half).start()

    def finish(step, carry):
        for path in range(2):
            peer = lax.rem(mines[path] + step, PEERS)
            home(path, peer, mines[path], peer).wait_send()
            home(path, mines[path], peer, peer).wait_recv()
            exchange(path, peer, mines[path], peer).wait_send()
        return carry

    lax.fori_loop(1, PEERS, finish, 0)
    own_a.wait()
    own_b.wait()

    def combine(path, owner):
        code = (code_a, code_b)[path]
        back = (back_a, back_b)[path]
        lanes = pl.ds(pl.multiple_of(owner * TOK, TOK), TOK)
        slot = lax.broadcasted_iota(jnp.int32, (BLOCK, TOK), 0).astype(F32)
        hot = jnp.concatenate(
            [
                jnp.where(code[k : k + 1, lanes] == slot, 1.0, 0.0).astype(BF)
                for k in range(PEERS)
            ],
            axis=0,
        )
        width = (LANES_A, LANES_B)[path]
        return lax.dot_general(
            hot, back[...].reshape(SLOTS, width), over_rows, preferred_element_type=F32
        )

    def sums(owner, carry):
        part_a[owner] = combine(0, owner).astype(BF)
        part_b[owner] = combine(1, owner).astype(BF)
        return carry

    lax.fori_loop(0, RING, sums, 0)

    loops = (
        (part_a, run_a, got_a, y, lambda v: (v * PEERS + z * 2 + core, dp)),
        (part_b, run_b, got_b, z, lambda v: (y * PEERS + v * 2 + core, dp)),
    )

    def halves(way, step):
        return (way,) if step == 0 else (0, 1)

    def hop(ring, way, step, half):
        part, run, got, at, device = loops[ring]
        sign = 1 if way == 0 else RING - 1
        rows = pl.ds(half * HALF, HALF)
        return pltpu.make_async_remote_copy(
            src_ref=run.at[way, step, rows],
            dst_ref=got.at[way, step, rows],
            send_sem=rs_send.at[ring, way, step, half],
            recv_sem=rs_recv.at[ring, way, step, half],
            device_id=device(lax.rem(at + sign, RING)),
            device_id_type=MESH,
        )

    for step in range(4):
        for half in range(2):
            for ring in range(2):
                part, run, got, at, device = loops[ring]
                rows = pl.ds(half * HALF, HALF)
                for way in range(2):
                    if half not in halves(way, step):
                        continue
                    sign = 1 if way == 0 else RING - 1
                    owner = lax.rem(at + sign * (4 - step), RING)
                    total = part[owner, rows]
                    if step > 0 and half in halves(way, step - 1):
                        hop(ring, way, step - 1, half).wait_recv()
                        total = (total.astype(F32) + got[way, step - 1, rows].astype(F32)).astype(BF)
                    run[way, step, rows] = total
                    hop(ring, way, step, half).start()
        if step == 0:
            for half in range(2):
                total = grads[half, dp].astype(F32)
                for way in range(2):
                    grad_hop(way, 1, half).wait_recv()
                    total = total + grad_got[way, 1, half].astype(F32)
                grad_ref[half] = total
    for half in range(2):
        for ring in range(2):
            part, run, got, at, device = loops[ring]
            rows = pl.ds(half * HALF, HALF)
            total = part[at, rows].astype(F32)
            for way in range(2):
                hop(ring, way, 3, half).wait_recv()
                total = total + got[way, 3, rows].astype(F32)
            (out_a, out_b)[ring][rows] = total.astype(BF)

    for step in range(4):
        for ring in range(2):
            for way in range(2):
                for half in range(2):
                    if sent(step, way, half):
                        piece(ring, way, step, half).wait_send()
                    if half in halves(way, step):
                        hop(ring, way, step, half).wait_send()
    for way in range(2):
        for half in range(2):
            weight_piece(way, 0, half).wait_send()
            grad_hop(way, 1, half).wait_send()
        weight_piece(way, 1, way).wait_send()
        grad_hop(way, 0, way).wait_send()


def layer(xa, cb, state, perm):
    vm = pl.BlockSpec(memory_space=pltpu.VMEM)
    sm = pl.BlockSpec(memory_space=pltpu.SMEM)
    hbm = pl.BlockSpec(memory_space=pl.ANY)
    dma = pltpu.SemaphoreType.DMA
    shape = jax.ShapeDtypeStruct
    n_dp = lax.axis_size("dp")
    count = PEERS * RING
    return pl.pallas_call(
        layer_kernel,
        out_shape=[
            shape((TOK, LANES_A), BF),
            shape((TOK, LANES_B), BF),
            shape((2, D // n_dp, FF), F32),
            shape((RING, RING, 16, FF), BF),
            shape((RING, RING, 16, FF), BF),
        ],
        in_specs=[vm, vm, vm, sm],
        out_specs=[vm] * 5,
        scratch_shapes=[
            pltpu.VMEM((RING, TOK, xa.shape[1]), BF),
            pltpu.VMEM((RING, TOK, cb.shape[1]), BF),
            pltpu.VMEM((PEERS, RING * TOK), F32),
            pltpu.VMEM((PEERS, RING * TOK), F32),
            pltpu.VMEM((PEERS, RING * TOK), F32),
        ]
        + [pltpu.VMEM((PEERS, BLOCK, D), BF)] * 4
        + [
            pltpu.VMEM((PEERS, RING, 16, FF), BF),
            pltpu.VMEM((count, 16, FF), BF),
            pltpu.VMEM((count, 16, FF), BF),
            pltpu.VMEM((RING, PEERS, 16, FF), BF),
            pltpu.VMEM((2, n_dp, D // n_dp, FF), BF),
            pltpu.VMEM((SLOTS, FF), BF),
            pltpu.VMEM((SLOTS, FF), BF),
            pltpu.VMEM((SLOTS, FF), F32),
            pltpu.VMEM((SLOTS, FF), BF),
            pltpu.VMEM((SLOTS, FF), BF),
            pltpu.VMEM((SLOTS, FF), BF),
            pltpu.VMEM((PEERS, BLOCK, LANES_A), BF),
            pltpu.VMEM((PEERS, BLOCK, LANES_B), BF),
            pltpu.VMEM((PEERS, BLOCK, LANES_A), BF),
            pltpu.VMEM((PEERS, BLOCK, LANES_B), BF),
            pltpu.VMEM((RING, TOK, LANES_A), BF),
            pltpu.VMEM((RING, TOK, LANES_B), BF),
            pltpu.VMEM((2, 4, TOK, LANES_A), BF),
            pltpu.VMEM((2, 4, TOK, LANES_B), BF),
            pltpu.VMEM((2, 4, TOK, LANES_A), BF),
            pltpu.VMEM((2, 4, TOK, LANES_B), BF),
            pltpu.VMEM((2, n_dp, D // n_dp, FF), BF),
            pltpu.VMEM((2, 2, D // n_dp, FF), BF),
            pltpu.VMEM((2, 2, 2, D // n_dp, FF), BF),
            dma((2, 2, 4, 2)),
            dma((2, 2, 4, 2)),
            dma((2, PEERS)),
            dma((2, PEERS)),
            dma((2, PEERS)),
            dma((2, PEERS)),
            dma((2, 2, 4, 2)),
            dma((2, 2, 4, 2)),
            dma((2, 4, PEERS)),
            dma((2, 4, PEERS)),
            dma((2, 4)),
            dma((2, 2, 2)),
            dma((2, 2, 2)),
            dma((2, 2, 2)),
            dma((2, 2, 2)),
            dma((2,)),
        ],
        compiler_params=pltpu.CompilerParams(
            collective_id=0, has_side_effects=True, vmem_limit_bytes=62 * 2**20
        ),
        name="layer",
    )(xa, cb, state, perm)


def moved(plan, index):
    gone = index[..., None]
    step = jnp.where(gone == plan[:, 0], plan[:, 1] - gone, 0) + jnp.where(
        gone == plan[:, 1], plan[:, 0] - gone, 0
    )
    return index + jnp.sum(step, axis=-1)


def adam_update(master, moment_one, moment_two, average, gradient):
    first = BETA_ONE * moment_one.astype(F32) + (1.0 - BETA_ONE) * gradient
    second = BETA_TWO * moment_two.astype(F32) + (1.0 - BETA_TWO) * gradient * gradient
    fresh = master - LEARN_RATE * first / (jnp.sqrt(second) + ADAM_EPS)
    smooth = EMA_DECAY * average.astype(F32) + (1.0 - EMA_DECAY) * fresh
    return (fresh, first.astype(BF), second.astype(BF), smooth.astype(BF))


def shards(
    tokens, expert_ids, gate_weights, cotangent, migration_plan,
    master, moment_one, moment_two, average,
):
    count = lax.axis_size("ep")
    me = lax.axis_index("ep")
    holder = moved(migration_plan, jnp.arange(count, dtype=jnp.int32))
    target = moved(migration_plan, expert_ids)

    shape = master.shape
    state = jnp.stack(
        [
            jnp.concatenate([v.astype(BF).reshape(-1, 16, FF) for v in pair]).reshape(RING, RING, 16, FF)
            for pair in ((master, moment_one), (moment_two, average))
        ]
    )
    stays = jnp.sum((migration_plan == me).astype(jnp.int32)) == 0
    turned = (lax.rem(holder, PEERS) // 2) * PEERS + (holder // PEERS) * 2 + lax.rem(holder, 2)
    turned = turned.reshape(RING, RING, 2).transpose(1, 0, 2).reshape(-1)
    perm = jnp.stack([holder, turned])

    columns = jnp.arange(count, dtype=jnp.int32)
    hits = columns[:, None, None] == target.T[None]
    chosen = jnp.any(hits, axis=1)
    gates = jnp.sum(jnp.where(hits, gate_weights.T[None], 0), axis=1).astype(BF)
    before = (jnp.arange(TOK)[:, None] < jnp.arange(TOK)[None, :]).astype(BF)
    rank = jnp.dot(chosen.astype(BF), before, preferred_element_type=F32)
    rank = jnp.where(chosen, rank, -1.0).astype(BF)

    def by_column(table):
        return table.reshape(RING, RING, 2, TOK).transpose(1, 0, 2, 3).reshape(count, TOK)

    xa = jnp.concatenate([tokens, rank], axis=1)
    cb = jnp.concatenate([cotangent, by_column(rank), by_column(gates)], axis=1)
    sum_a, sum_b, grad, fin_r, fin_c = layer(xa, cb, state, perm)
    weights, moment_one = (v.reshape(shape) for v in jnp.split(fin_r, 2))
    moment_two, average = (v.reshape(shape) for v in jnp.split(fin_c, 2))
    master = jnp.where(stays, master, weights.astype(F32))
    grad = grad[None]
    new_master, first, second, smooth = adam_update(master, moment_one, moment_two, average, grad)
    token_grad = jnp.concatenate([sum_a[:, : LANES_A - TOK], sum_b], axis=1)
    gate_sums = sum_a[:, LANES_A - TOK :].astype(F32)
    picked = jnp.sum(
        jnp.where(target[:, :, None] == columns[None, None, :], gate_sums[:, None, :], 0.0), axis=2
    )
    gate_grad = (picked / gate_weights.astype(F32)).astype(BF)
    return (token_grad, gate_grad, new_master, first, second, smooth)


def solution(mesh):
    rows = P(("ep", "dp"), None)
    held = P("ep", None, "dp", None)
    return jax.shard_map(
        shards,
        mesh=mesh,
        in_specs=(rows, rows, rows, rows, P(), held, held, held, held),
        out_specs=(rows, rows, held, held, held, held),
        check_vma=False,
    )
```

time: 334 us -> 301 us (0.901)
  Pallas kernels: 185 us -> 279 us
  blocking collectives: 48.7 us -> 0 us
  waiting for transfers between devices: 41 us -> 0 us
  starting transfers between devices: 18.8 us -> 0 us
  between operations: 14.9 us -> 1.49 us
  matrix products: 4.6 us -> 0.14 us
    pallas_call x3 -> x1, Pallas kernels: 185 us -> 279 us  [layer(): pl.pallas_call(layer_kernel, out_shape=[shape((TOK, LANES_A), BF), shape(...]
    all_to_all x1 -> x0, blocking collectives: 48.7 us -> none  [relocate(): lax.all_to_all(arranged, 'ep', split_axis=0, concat_axis=0, tiled=True)]
    all_to_all x1 -> x0, waiting for transfers between devices: 40.9 us -> none  [relocate(): lax.all_to_all(state, 'ep', split_axis=0, concat_axis=0, tiled=True)]
    all_to_all x1 -> x0, starting transfers between devices: 18.6 us -> none  [relocate(): lax.all_to_all(state, 'ep', split_axis=0, concat_axis=0, tiled=True)]
    dot_general x2 -> x0, matrix products: 4.45 us -> none  [the longest x1 2.9 us: shards(): lax.dot_general(xr, act_grad, over_rows, preferred_element_type=F32)]
  transfers between devices with their start and end apart: 3 -> 0, of which waited for: 1 -> 0; matrix products, arithmetic and copies ran while one was open for 3% -> 0% of each run, Pallas kernels for 50% -> 0%
where the time goes in v2:
time: 301 us
  Pallas kernels  279 us (93%)
  other arithmetic  17 us (6%)
    pallas_call x1, Pallas kernels, layer(): pl.pallas_call(layer_kernel, out_shape=[shape((TOK, LANES_A), BF), shape(...  279 us

profile of v2, /device:TPU:1, one launch (start us, length us, event | category | flops | bytes accessed | tf_op | source)
XLA Modules:
  0.0 300.7 jit_solution(15560688611567440519)
XLA Ops:
  0.6 0.0 copy-start.3
  0.6 0.0 copy-start.4
  0.7 0.0 copy-start
  0.7 0.8 slice_bitcast_fusion.1
  1.5 0.8 add_reduce_fusion
  2.3 0.7 add.55
  2.9 0.2 fusion.4
  3.1 0.1 fusion
  3.3 1.7 pad_maximum_fusion.4.xa_ref
  5.0 0.9 fusion.5
  5.9 0.0 copy-start.5
  5.9 1.8 pad_maximum_fusion.3.cb_ref
  7.7 0.0 copy-done.3
  7.7 0.0 copy-done.4
  7.7 0.1 pad_maximum_fusion.2
  7.8 0.0 copy-done
  7.8 0.0 copy-done.5
  7.8 0.1 pad_maximum_fusion.1
  7.9 1.3 pad_maximum_fusion.state
  9.3 0.1 add_reduce_fusion.1
  9.4 0.1 reduce_sum.56
  9.5 0.1 fusion.10
  9.6 0.1 stack_reshape.11
  9.7 0.6 pad_add_fusion.perm
  10.3 0.0 copy-start.6
  10.3 279.0 %layer.1 = (bf16[128,640]{1,0:T(8,128)(2,1)}, bf16[128,512]{1,0:T(8,128)(2,1)}, f32[2,256,384]{2,1,0:T(8,128)}, bf16[8,8,16,384]{3,2,1,0:T(8,128)(2,1)}, bf16[8,8,16,384]{3,2,1,0:T(8,128)(2,1)}) custom-call(bf16[128,1152]{1,0:T(8,128)(2,1)} %pad_maximum_fusion.4.xa_ref, bf16[128,1280]{1,0:T(8,128)(2,1)} %pad_maximum_fusion.3.cb_ref, ...), custom_call_target="tpu_custom_call" | custom-call | tf_op jit(solution)/shard_map/layer/pallas_call | solution.py:607
  289.3 0.9 slice.20
  290.2 1.6 pad_maximum_fusion.5
  291.9 0.8 slice_convert_fusion
  292.6 0.1 copy.27
  292.7 0.4 select_reduce_fusion
  293.1 0.0 copy-done.6
  293.1 0.1 copy.28
  293.2 0.7 copy.29
  293.9 0.0 copy-start.2
  293.9 0.0 copy-start.7
  293.9 1.5 convert_multiply_fusion.1
  295.5 0.0 copy-done.2
  295.5 0.0 copy-done.7
  295.5 0.6 fusion.15
  296.8 0.0 copy-start.1
  296.8 2.8 add_convert_fusion
  299.6 0.0 copy-done.1
  299.6 1.1 convert_bitcast_fusion
  (7 shorter events, 0.2 us)
Async XLA Ops:
  0.6 7.0 %copy-start.3 = (bf16[1,2,256,384]{3,2,1,0:T(8,128)(2,1)S(1)}, bf16[1,2,256,384]{3,2,1,0:T(8,128)(2,1)}, u32[]{:S(2)}) copy-start(bf16[1,2,256,384]{3,2,1,0:T(8,128)(2,1)} %param.17) | copy-start | bytes 1179652
  0.6 7.0 %copy-start.4 = (bf16[1,2,256,384]{3,2,1,0:T(8,128)(2,1)S(1)}, bf16[1,2,256,384]{3,2,1,0:T(8,128)(2,1)}, u32[]{:S(2)}) copy-start(bf16[1,2,256,384]{3,2,1,0:T(8,128)(2,1)} %param.16) | copy-start | bytes 1179652
  0.7 7.1 %copy-start = (f32[1,2,256,384]{3,2,1,0:T(8,128)S(1)}, f32[1,2,256,384]{3,2,1,0:T(8,128)}, u32[]{:S(2)}) copy-start(f32[1,2,256,384]{3,2,1,0:T(8,128)} %param.14) | copy-start | bytes 2359300
  5.9 1.9 copy-start.5
  10.3 282.8 %copy-start.6 = (bf16[128,8]{0,1:T(8,128)(2,1)S(1)}, bf16[128,8]{0,1:T(8,128)(2,1)}, u32[]{:S(2)}) copy-start(bf16[128,8]{0,1:T(8,128)(2,1)} %param.11) | copy-start | bytes 6148
  293.9 1.6 copy-start.2
  293.9 1.6 copy-start.7
  296.8 2.8 copy-start.1

commit v3 on v2

--- a/solution.py
+++ b/solution.py
@@ -67,15 +67,15 @@
 
 
 def layer_kernel(
-    xa_ref, cb_ref, state, perm,
-    out_a, out_b, grad_ref, fin_r, fin_c,
+    xa_ref, cb_ref, state, lookup,
+    out_a, out_b, grad_ref, fin_w, fin_m,
     xall, call, code_a, code_b, gate, xs, cs, xr, sr,
-    s1, s2, arr, g1,
+    here, both, slots, run_m, got_m, out_m,
     wts, hg_hi, hg_lo, act_ref, hid, ag, hid_b,
-    pay_a, pay_b, back_a, back_b, part_a, part_b,
+    pay_a, pay_b, back_a, back_b,
     run_a, run_b, got_a, got_b, grads, grad_run, grad_got,
     ag_send, ag_recv, out_send, out_recv, home_send, home_recv, rs_send, rs_recv,
-    mig_send, mig_recv, mig_local, wt_send, wt_recv, gr_send, gr_recv, local,
+    mig_send, mig_recv, mig_local, mr_send, mr_recv, wt_send, wt_recv, gr_send, gr_recv, local,
 ):
     dp, y, z, core = place()
     me = lax.axis_index("ep")
@@ -125,117 +125,175 @@
     def sent(step, way, half):
         return step < 3 or way == half
 
-    firsts, seconds = (z, y), (y, z)
-
-    def mig_plan(which, stage):
-        if stage in (0, 3):
-            to = (
-                (lambda s: (y * PEERS + s, dp)) if which == 0
-                else (lambda s: ((s // 2) * PEERS + z * 2 + lax.rem(s, 2), dp))
-            )
-        else:
-            to = (
-                (lambda v: (v * PEERS + z * 2 + core, dp)) if which == 0
-                else (lambda v: (y * PEERS + v * 2 + core, dp))
-            )
+    mig_device = (col_of, row_of)
+    mig_mine = (col_mine, row_mine)
+    mig_at = (z, y)
+    mig_ring = (
+        lambda v: (y * PEERS + v * 2 + core, dp),
+        lambda v: (v * PEERS + z * 2 + core, dp),
+    )
+
+    def mig_ends(which, stage, peer, slot):
         if stage == 0:
-            src = (lambda u: state.at[0, :, u]) if which == 0 else (lambda u: state.at[1, u])
-            return (lambda u: to(u * 2 + which)), src, (lambda s: s1.at[s])
+            return state.at[:, which, peer], here.at[which, slot]
         if stage == 1:
-            return to, (lambda v: s1.at[:, v]), (lambda v: s2.at[pl.ds(v * PEERS, PEERS)])
-        if stage == 2:
-            return to, (lambda v: arr.at[pl.ds(v * PEERS, PEERS)]), (lambda v: g1.at[v])
-        dst = (lambda u: fin_r.at[:, u]) if which == 0 else (lambda u: fin_c.at[u])
-        return to, (lambda s: g1.at[:, s]), dst
-
-    def migrate(which, stage, peer, place_there):
-        to, src, dst = mig_plan(which, stage)
+            return out_m.at[which, peer, pl.ds(0, 1)], fin_w.at[:, which, slot]
+        return out_m.at[which, peer, pl.ds(1, 3)], fin_m.at[:, which, slot]
+
+    def mig_move(which, stage, peer, slot):
+        src, dst = mig_ends(which, stage, peer, slot)
         return pltpu.make_async_remote_copy(
-            src_ref=src(peer),
-            dst_ref=dst(place_there),
+            src_ref=src,
+            dst_ref=dst,
             send_sem=mig_send.at[which, stage, peer],
-            recv_sem=mig_recv.at[which, stage, place_there],
-            device_id=to(peer),
+            recv_sem=mig_recv.at[which, stage, slot],
+            device_id=mig_device[which](peer),
             device_id_type=MESH,
         )
 
     def mig_own(which, stage):
-        _, src, dst = mig_plan(which, stage)
-        here = (
-            (firsts[which], mines[which]),
-            (seconds[which], seconds[which]),
-            (seconds[which], seconds[which]),
-            (mines[which], firsts[which]),
-        )[stage]
-        return pltpu.make_async_copy(src(here[0]), dst(here[1]), mig_local.at[which, stage])
-
-    def mig_sends(which, stage, act):
-        if stage == 0:
-            first = firsts[which]
-
-            def go(step, carry):
-                act(lax.rem(first + step, RING), mines[which])
-                return carry
-
-            lax.fori_loop(1, RING, go, 0)
-
-            @pl.when(core != which)
-            def _():
-                act(first, mines[which])
-        else:
-            count, at, slot = (
-                (PEERS, mines[which], firsts[which]) if stage == 3
-                else (RING, seconds[which], seconds[which])
-            )
-
-            @pl.when(core == which)
-            def _():
-                def go(step, carry):
-                    act(lax.rem(at + step, count), slot)
-                    return carry
-
-                lax.fori_loop(1, count, go, 0)
+        mine = mig_mine[which]
+        src, dst = mig_ends(which, stage, mine, mine)
+        return pltpu.make_async_copy(src, dst, mig_local.at[which, stage])
 
     def mig_start(stage):
+        def go(step, carry):
+            for which in range(2):
+                mine = mig_mine[which]
+                mig_move(which, stage, lax.rem(mine + step, PEERS), mine).start()
+            return carry
+
+        lax.fori_loop(1, PEERS, go, 0)
         for which in range(2):
-            mig_sends(which, stage, lambda peer, slot: migrate(which, stage, peer, slot).start())
-
-            @pl.when(core == which)
-            def _():
-                mig_own(which, stage).start()
+            mig_own(which, stage).start()
 
     def mig_wait(stage):
+        def hold(step, carry):
+            for which in range(2):
+                mine = mig_mine[which]
+                peer = lax.rem(mine + step, PEERS)
+                mig_move(which, stage, peer, mine).wait_send()
+                mig_move(which, stage, peer, peer).wait_recv()
+            return carry
+
+        lax.fori_loop(1, PEERS, hold, 0)
         for which in range(2):
-            mig_sends(which, stage, lambda peer, slot: migrate(which, stage, peer, slot).wait_send())
-            if stage == 3:
-                first = firsts[which]
-
-                def hold(step, carry):
-                    migrate(which, stage, mines[which], lax.rem(first + step, RING)).wait_recv()
-                    return carry
-
-                lax.fori_loop(1, RING, hold, 0)
-
-                @pl.when(core != which)
-                def _():
-                    migrate(which, stage, mines[which], first).wait_recv()
-
-                @pl.when(core == which)
-                def _():
-                    mig_own(which, stage).wait()
-            else:
-                count, at = (PEERS, mines[which]) if stage == 0 else (RING, seconds[which])
-
-                @pl.when(core == which)
-                def _():
-                    def hold(step, carry):
-                        slot = lax.rem(at + step, count)
-                        peer = firsts[which] if stage == 0 else slot
-                        migrate(which, stage, peer, slot).wait_recv()
-                        return carry
-
-                    lax.fori_loop(1, count, hold, 0)
-                    mig_own(which, stage).wait()
+            mig_own(which, stage).wait()
+
+    def mig_pick():
+        def one(k, carry):
+            for which in range(2):
+                for j in range(2):
+                    slots[which, k, j] = here[which, lookup[which, 2 * k + j]]
+            return carry
+
+        for which in range(2):
+            here[which, PEERS] = jnp.zeros(here.shape[2:], BF)
+        lax.fori_loop(0, RING, one, 0)
+
+    def mig_hop(which, way, step):
+        sign = 1 if way == 0 else RING - 1
+        span = pl.ds(way, 1) if step == 0 else pl.ds(0, 2)
+        return pltpu.make_async_remote_copy(
+            src_ref=run_m.at[which, way, step, span],
+            dst_ref=got_m.at[which, way, step, span],
+            send_sem=mr_send.at[0, which, way, step],
+            recv_sem=mr_recv.at[0, which, way, step],
+            device_id=mig_ring[which](lax.rem(mig_at[which] + sign, RING)),
+            device_id_type=MESH,
+        )
+
+    def mig_sum(step):
+        for which in range(2):
+            for way in range(2):
+                sign = 1 if way == 0 else RING - 1
+                owner = lax.rem(mig_at[which] + sign * (4 - step), RING)
+                if step > 0:
+                    mig_hop(which, way, step - 1).wait_recv()
+                for j in range(2):
+                    if step == 0 and j != way:
+                        continue
+                    total = slots[which, owner, j]
+                    if step > 1 or (step == 1 and j == way):
+                        total = total + got_m[which, way, step - 1, j]
+                    run_m[which, way, step, j] = total
+                mig_hop(which, way, step).start()
+
+    def mig_own_slots():
+        for which in range(2):
+            at = mig_at[which]
+            total = slots[which, at]
+            for way in range(2):
+                mig_hop(which, way, 3).wait_recv()
+                total = total + got_m[which, way, 3]
+            both[which, pl.ds(PEERS + 2 * at, 2)] = total
+
+    def mig_spread(which, way, step, arriving=False):
+        back = step + 1 if arriving else step
+        sign = 1 if way == 0 else RING - 1
+        source = lax.rem(mig_at[which] + (RING - sign) * back, RING)
+        first = PEERS + 2 * source
+        part = both.at[which, pl.ds(first + way, 1) if step == 3 else pl.ds(first, 2)]
+        return pltpu.make_async_remote_copy(
+            src_ref=part,
+            dst_ref=part,
+            send_sem=mr_send.at[1, which, way, step],
+            recv_sem=mr_recv.at[1, which, way, step],
+            device_id=mig_ring[which](lax.rem(mig_at[which] + sign, RING)),
+            device_id_type=MESH,
+        )
+
+    def mig_gather(step):
+        for which in range(2):
+            for way in range(2):
+                if step > 0:
+                    mig_spread(which, way, step - 1, True).wait_recv()
+                if step < 4:
+                    mig_spread(which, way, step).start()
+
+    def mig_place():
+        for which in range(2):
+            both[which, 0:PEERS] = here[which, 0:PEERS]
+
+        def one(p, carry):
+            for which in range(2):
+                out_m[which, p] = both[which, lookup[2 + which, p]]
+            return carry
+
+        lax.fori_loop(0, PEERS, one, 0)
+
+    def mig_end():
+        mig_wait(2)
+        for which in range(2):
+            for way in range(2):
+                for step in range(4):
+                    mig_hop(which, way, step).wait_send()
+                    mig_spread(which, way, step).wait_send()
+
+    def weight_piece(way, step, half, arriving=False):
+        back = step + 1 if arriving else step
+        sign = 1 if way == 0 else 3
+        source = lax.rem(dp + (4 - sign) * back, n_dp)
+        part = wts.at[half, source]
+        return pltpu.make_async_remote_copy(
+            src_ref=part,
+            dst_ref=part,
+            send_sem=wt_send.at[way, step, half],
+            recv_sem=wt_recv.at[way, step, half],
+            device_id=(me, lax.rem(dp + sign, n_dp)),
+            device_id_type=MESH,
+        )
+
+    def weights_out():
+        for half in range(2):
+            wts[half, dp] = fin_w[0, half].reshape(D // 4, FF)
+            for way in range(2):
+                weight_piece(way, 0, half).start()
+
+    def weights_on():
+        for way in range(2):
+            weight_piece(way, 0, way, True).wait_recv()
+            weight_piece(way, 1, way).start()
 
     for step in range(4):
         for half in range(2):
@@ -246,10 +304,16 @@
                     if sent(step, way, half):
                         piece(ring, way, step, half).start()
         if step == 0:
-            mig_start(0)
             for ring in range(2):
                 own, everyone, at, device = rings[ring]
                 everyone[at] = own[...]
+        if step == 0:
+            mig_start(0)
+        elif step == 1:
+            mig_wait(0)
+            mig_pick()
+        if step > 0:
+            mig_sum(step - 1)
     for ring in range(2):
         for way in range(2):
             piece(ring, way, 3, way, True).wait_recv()
@@ -295,50 +359,42 @@
         rows = jnp.dot(hot, table, preferred_element_type=F32).astype(BF)
         buffer = (xs, cs)[path]
         buffer[pl.ds(first, group)] = rows.reshape(group, BLOCK, D)
-        for k in range(group):
+
+    def issue(path, step, low, high):
+        mine = mines[path]
+        first = lax.rem(mine // group + step, n_group) * group
+        for k in range(low, high):
             peer = first + k
 
             @pl.when(peer != mine)
             def _():
                 exchange(path, peer, mine, peer).start()
 
-    def weight_piece(way, step, half, arriving=False):
-        back = step + 1 if arriving else step
-        sign = 1 if way == 0 else 3
-        source = lax.rem(dp + (4 - sign) * back, n_dp)
-        part = wts.at[half, source]
-        return pltpu.make_async_remote_copy(
-            src_ref=part,
-            dst_ref=part,
-            send_sem=wt_send.at[way, step, half],
-            recv_sem=wt_recv.at[way, step, half],
-            device_id=(me, lax.rem(dp + sign, n_dp)),
-            device_id_type=MESH,
-        )
-
-    def reorder(p, carry):
-        arr[p] = s2[perm[core, p]]
-        return carry
-
+    mig_sum(3)
+    early = 1
+    for step in range(4):
+        if step == 0:
+            mig_own_slots()
+        mig_gather(step)
+        build(step % 2, step // 2)
+        issue(step % 2, step // 2, 0, early)
+    mig_gather(4)
+    mig_place()
+    mig_start(1)
+    mig_start(2)
     for step in range(n_group):
-        build(0, step)
-        build(1, step)
-        mig_wait(step)
-        if step == 1:
-            lax.fori_loop(0, PEERS * RING, reorder, 0)
-        if step < 3:
-            mig_start(step + 1)
-    for half in range(2):
-        wts[half, dp] = fin_r[half * 2 : half * 2 + 2].reshape(D // 4, FF)
-        for way in range(2):
-            weight_piece(way, 0, half).start()
+        for path in range(2):
+            if step > 1:
+                build(path, step)
+            issue(path, step, early if step < 2 else 0, group)
+        if step == 2:
+            mig_wait(1)
+            weights_out()
     own_a = pltpu.make_async_copy(xs.at[row_mine], xr.at[row_mine], local.at[0])
     own_b = pltpu.make_async_copy(cs.at[col_mine], sr.at[col_mine], local.at[1])
     own_a.start()
     own_b.start()
-    for way in range(2):
-        weight_piece(way, 0, way, True).wait_recv()
-        weight_piece(way, 1, way).start()
+    weights_on()
     for way in range(2):
         weight_piece(way, 0, 1 - way, True).wait_recv()
         weight_piece(way, 1, way, True).wait_recv()
@@ -355,7 +411,7 @@
     def flat(first):
         return pl.ds(pl.multiple_of(first * BLOCK, rows_per), rows_per)
 
-    def project(step, carry):
+    def project(step):
         for path in range(2):
             mine = mines[path]
             first = lax.rem(mine // group + n_group - step, n_group) * group
@@ -377,9 +433,9 @@
                 hi = hg.astype(BF)
                 hg_hi[flat(first), :] = hi
                 hg_lo[flat(first), :] = (hg - hi.astype(F32)).astype(BF)
-        return carry
-
-    lax.fori_loop(0, n_group, project, 0)
+
+    for step in range(n_group):
+        project(step)
 
     def home(path, slot_here, slot_there, peer):
         src, dst, device = ((pay_a, back_a, row_of), (pay_b, back_b, col_of))[path]
@@ -405,7 +461,7 @@
 
     width_a = LANES_A - TOK
 
-    def backward(step, carry):
+    def backward(step):
         first = lax.rem(row_mine // group + step, n_group) * group
         rows = flat(first)
         swap = swaps(first)
@@ -430,11 +486,11 @@
             jnp.where(lane == me, gates, 0.0).astype(BF).reshape(group, BLOCK, TOK)
         )
         send_home(0, first)
-        return carry
-
-    lax.fori_loop(0, n_group, backward, 0)
-
-    def swapped(step, carry):
+
+    for step in range(n_group):
+        backward(step)
+
+    def swapped(step):
         first = lax.rem(col_mine // group + step, n_group) * group
         rows = flat(first)
         swap = swaps(first)
@@ -446,9 +502,9 @@
         )
         pay_b[pl.ds(first, group)] = pair.astype(BF).reshape(group, BLOCK, LANES_B)
         send_home(1, first)
-        return carry
-
-    lax.fori_loop(0, n_group, swapped, 0)
+
+    for step in range(n_group):
+        swapped(step)
     own_a = pltpu.make_async_copy(pay_a.at[row_mine], back_a.at[row_mine], local.at[0])
     own_b = pltpu.make_async_copy(pay_b.at[col_mine], back_b.at[col_mine], local.at[1])
     own_a.start()
@@ -519,16 +575,23 @@
             hot, back[...].reshape(SLOTS, width), over_rows, preferred_element_type=F32
         )
 
+    for step in range(4):
+        for ring in range(2):
+            for way in range(2):
+                for half in range(2):
+                    if sent(step, way, half):
+                        piece(ring, way, step, half).wait_send()
+
     def sums(owner, carry):
-        part_a[owner] = combine(0, owner).astype(BF)
-        part_b[owner] = combine(1, owner).astype(BF)
+        xall[owner, :, :LANES_A] = combine(0, owner).astype(BF)
+        call[owner, :, :LANES_B] = combine(1, owner).astype(BF)
         return carry
 
     lax.fori_loop(0, RING, sums, 0)
 
     loops = (
-        (part_a, run_a, got_a, y, lambda v: (v * PEERS + z * 2 + core, dp)),
-        (part_b, run_b, got_b, z, lambda v: (y * PEERS + v * 2 + core, dp)),
+        (xall, run_a, got_a, y, lambda v: (v * PEERS + z * 2 + core, dp)),
+        (call, run_b, got_b, z, lambda v: (y * PEERS + v * 2 + core, dp)),
     )
 
     def halves(way, step):
@@ -557,7 +620,7 @@
                         continue
                     sign = 1 if way == 0 else RING - 1
                     owner = lax.rem(at + sign * (4 - step), RING)
-                    total = part[owner, rows]
+                    total = part[owner, rows, : run.shape[-1]]
                     if step > 0 and half in halves(way, step - 1):
                         hop(ring, way, step - 1, half).wait_recv()
                         total = (total.astype(F32) + got[way, step - 1, rows].astype(F32)).astype(BF)
@@ -574,20 +637,18 @@
         for ring in range(2):
             part, run, got, at, device = loops[ring]
             rows = pl.ds(half * HALF, HALF)
-            total = part[at, rows].astype(F32)
+            total = part[at, rows, : run.shape[-1]].astype(F32)
             for way in range(2):
                 hop(ring, way, 3, half).wait_recv()
                 total = total + got[way, 3, rows].astype(F32)
             (out_a, out_b)[ring][rows] = total.astype(BF)
 
+    mig_end()
     for step in range(4):
         for ring in range(2):
             for way in range(2):
-                for half in range(2):
-                    if sent(step, way, half):
-                        piece(ring, way, step, half).wait_send()
-                    if half in halves(way, step):
-                        hop(ring, way, step, half).wait_send()
+                for half in halves(way, step):
+                    hop(ring, way, step, half).wait_send()
     for way in range(2):
         for half in range(2):
             weight_piece(way, 0, half).wait_send()
@@ -596,7 +657,7 @@
         grad_hop(way, 0, way).wait_send()
 
 
-def layer(xa, cb, state, perm):
+def layer(xa, cb, state, lookup):
     vm = pl.BlockSpec(memory_space=pltpu.VMEM)
     sm = pl.BlockSpec(memory_space=pltpu.SMEM)
     hbm = pl.BlockSpec(memory_space=pl.ANY)
@@ -610,11 +671,11 @@
             shape((TOK, LANES_A), BF),
             shape((TOK, LANES_B), BF),
             shape((2, D // n_dp, FF), F32),
-            shape((RING, RING, 16, FF), BF),
-            shape((RING, RING, 16, FF), BF),
+            shape((1, 2, PEERS, 16, FF), BF),
+            shape((3, 2, PEERS, 16, FF), BF),
         ],
-        in_specs=[vm, vm, vm, sm],
-        out_specs=[vm] * 5,
+        in_specs=[vm, vm, hbm, sm],
+        out_specs=[vm] * 4 + [hbm],
         scratch_shapes=[
             pltpu.VMEM((RING, TOK, xa.shape[1]), BF),
             pltpu.VMEM((RING, TOK, cb.shape[1]), BF),
@@ -624,10 +685,17 @@
         ]
         + [pltpu.VMEM((PEERS, BLOCK, D), BF)] * 4
         + [
-            pltpu.VMEM((PEERS, RING, 16, FF), BF),
-            pltpu.VMEM((count, 16, FF), BF),
-            pltpu.VMEM((count, 16, FF), BF),
-            pltpu.VMEM((RING, PEERS, 16, FF), BF),
+            pltpu.VMEM(dims, BF)
+            for dims in (
+                (2, PEERS + 1, 4, 16, FF),
+                (2, 2 * PEERS, 4, 16, FF),
+                (2, RING, 2, 4, 16, FF),
+                (2, 2, 4, 2, 4, 16, FF),
+                (2, 2, 4, 2, 4, 16, FF),
+                (2, PEERS, 4, 16, FF),
+            )
+        ]
+        + [
             pltpu.VMEM((2, n_dp, D // n_dp, FF), BF),
             pltpu.VMEM((SLOTS, FF), BF),
             pltpu.VMEM((SLOTS, FF), BF),
@@ -639,8 +707,6 @@
             pltpu.VMEM((PEERS, BLOCK, LANES_B), BF),
             pltpu.VMEM((PEERS, BLOCK, LANES_A), BF),
             pltpu.VMEM((PEERS, BLOCK, LANES_B), BF),
-            pltpu.VMEM((RING, TOK, LANES_A), BF),
-            pltpu.VMEM((RING, TOK, LANES_B), BF),
             pltpu.VMEM((2, 4, TOK, LANES_A), BF),
             pltpu.VMEM((2, 4, TOK, LANES_B), BF),
             pltpu.VMEM((2, 4, TOK, LANES_A), BF),
@@ -656,9 +722,11 @@
             dma((2, PEERS)),
             dma((2, 2, 4, 2)),
             dma((2, 2, 4, 2)),
-            dma((2, 4, PEERS)),
-            dma((2, 4, PEERS)),
-            dma((2, 4)),
+            dma((2, 3, PEERS)),
+            dma((2, 3, PEERS)),
+            dma((2, 3)),
+            dma((2, 2, 2, 4)),
+            dma((2, 2, 2, 4)),
             dma((2, 2, 2)),
             dma((2, 2, 2)),
             dma((2, 2, 2)),
@@ -669,7 +737,7 @@
             collective_id=0, has_side_effects=True, vmem_limit_bytes=62 * 2**20
         ),
         name="layer",
-    )(xa, cb, state, perm)
+    )(xa, cb, state, lookup)
 
 
 def moved(plan, index):
@@ -694,20 +762,29 @@
 ):
     count = lax.axis_size("ep")
     me = lax.axis_index("ep")
-    holder = moved(migration_plan, jnp.arange(count, dtype=jnp.int32))
     target = moved(migration_plan, expert_ids)
 
     shape = master.shape
     state = jnp.stack(
-        [
-            jnp.concatenate([v.astype(BF).reshape(-1, 16, FF) for v in pair]).reshape(RING, RING, 16, FF)
-            for pair in ((master, moment_one), (moment_two, average))
-        ]
+        [v.astype(BF).reshape(2, PEERS, 16, FF) for v in (master, moment_one, moment_two, average)]
     )
-    stays = jnp.sum((migration_plan == me).astype(jnp.int32)) == 0
-    turned = (lax.rem(holder, PEERS) // 2) * PEERS + (holder // PEERS) * 2 + lax.rem(holder, 2)
-    turned = turned.reshape(RING, RING, 2).transpose(1, 0, 2).reshape(-1)
-    perm = jnp.stack([holder, turned])
+    entries = migration_plan.reshape(-1)
+    stays = jnp.sum((entries == me).astype(jnp.int32)) == 0
+    y = me // PEERS
+    z = lax.rem(me, PEERS) // 2
+    spot = jnp.arange(PEERS, dtype=jnp.int32)
+    columns_at = (entries // PEERS) * 2 + lax.rem(entries, 2)
+    take_up = jnp.where(lax.rem(entries, PEERS) // 2 == z, columns_at, PEERS)
+    take_down = jnp.where(entries // PEERS == y, lax.rem(entries, PEERS), PEERS)
+
+    def source(device):
+        old = moved(migration_plan, device)
+        slot = jnp.sum(jnp.where(old[:, None] == entries[None], spot[None], 0), axis=1)
+        return jnp.where(old == device, spot, PEERS + slot)
+
+    put_up = source((spot // 2) * PEERS + z * 2 + lax.rem(spot, 2))
+    put_down = source(y * PEERS + spot)
+    lookup = jnp.stack([take_up, take_down, put_up, put_down])
 
     columns = jnp.arange(count, dtype=jnp.int32)
     hits = columns[:, None, None] == target.T[None]
@@ -722,9 +799,9 @@
 
     xa = jnp.concatenate([tokens, rank], axis=1)
     cb = jnp.concatenate([cotangent, by_column(rank), by_column(gates)], axis=1)
-    sum_a, sum_b, grad, fin_r, fin_c = layer(xa, cb, state, perm)
-    weights, moment_one = (v.reshape(shape) for v in jnp.split(fin_r, 2))
-    moment_two, average = (v.reshape(shape) for v in jnp.split(fin_c, 2))
+    sum_a, sum_b, grad, weights, moments = layer(xa, cb, state, lookup)
+    weights = weights.reshape(shape)
+    moment_one, moment_two, average = (moments[k].reshape(shape) for k in range(3))
     master = jnp.where(stays, master, weights.astype(F32))
     grad = grad[None]
     new_master, first, second, smooth = adam_update(master, moment_one, moment_two, average, grad)

time: 301 us -> 253 us (0.84)
  Pallas kernels: 279 us -> 230 us
    pallas_call x1, Pallas kernels: 279 us -> 230 us  [layer(): pl.pallas_call(layer_kernel, out_shape=[shape((TOK, LANES_A), BF), shape(...]
where the time goes in v3:
time: 253 us; the launch traced here: 252 us
  Pallas kernels  230 us (91%)
  other arithmetic  15.5 us (6%)
  local copies, waits for them, and re-layouts  5.19 us (2%)
    pallas_call x1, Pallas kernels, layer(): pl.pallas_call(layer_kernel, out_shape=[shape((TOK, LANES_A), BF), shape(...  230 us

profile of v3, /device:TPU:1, one launch (start us, length us, event | category | flops | bytes accessed | tf_op | source)
XLA Modules:
  0.0 252.4 jit_solution(3482458211617254353)
XLA Ops:
  0.6 0.0 copy-start
  0.6 0.0 copy-start.3
  0.7 0.0 copy-start.4
  0.7 0.0 copy-start.5
  0.7 1.4 fusion.7
  2.8 0.8 slice_bitcast_fusion.1
  3.6 0.1 add_reduce_fusion.2
  3.7 0.8 add_reduce_fusion
  4.5 0.7 add.203
  5.2 0.8 copy.28
  5.9 0.1 reshape.383
  6.0 0.1 eq.192
  6.1 0.2 select_reduce_fusion.2
  6.3 0.6 pad_add_fusion.lookup
  6.9 0.2 fusion.5
  7.1 0.1 fusion
  7.3 0.9 fusion.6
  8.2 0.1 copy.30
  8.3 0.8 copy.31
  9.1 1.7 pad_maximum_fusion.1.cb_ref
  10.8 1.7 pad_maximum_fusion.2.xa_ref
  12.4 0.0 copy-done
  12.5 0.0 copy-done.3
  12.5 0.0 copy-done.4
  12.5 0.0 copy-done.5
  12.5 1.4 pad_maximum_fusion.state
  13.9 230.1 %layer.1 = (bf16[128,640]{1,0:T(8,128)(2,1)}, bf16[128,512]{1,0:T(8,128)(2,1)}, f32[2,256,384]{2,1,0:T(8,128)}, bf16[1,2,16,16,384]{4,3,2,1,0:T(8,128)(2,1)}, bf16[3,2,16,16,384]{4,3,2,1,0:T(8,128)(2,1)}) custom-call(bf16[128,1152]{1,0:T(8,128)(2,1)} %pad_maximum_fusion.2.xa_ref, bf16[128,1280]{1,0:T(8,128)(2,1)} %pad_maximum_fusion.1.cb_ref, ...), custom_call_target="tpu_custom_call" | custom-call | tf_op jit(solution)/shard_map/layer/pallas_call | solution.py:668
  244.0 0.0 copy-start.2
  244.0 0.9 slice_convert_fusion
  244.9 0.4 select_reduce_fusion
  245.3 0.9 slice.16
  246.2 0.7 copy.32
  246.8 1.6 pad_maximum_fusion.3
  248.5 0.0 copy-done.2
  248.5 0.0 copy-start.1
  248.5 0.0 copy-start.6
  248.5 0.2 convert_multiply_fusion.2
  248.7 0.9 copy-done.1
  249.6 0.1 copy-done.6
  249.7 1.6 fusion.3
  251.3 1.1 convert_bitcast_fusion
  (11 shorter events, 0.2 us)
Async XLA Ops:
  0.6 11.8 %copy-start = (f32[1,2,256,384]{3,2,1,0:T(8,128)S(1)}, f32[1,2,256,384]{3,2,1,0:T(8,128)}, u32[]{:S(2)}) copy-start(f32[1,2,256,384]{3,2,1,0:T(8,128)} %param.14) | copy-start | bytes 2359300
  0.6 11.9 %copy-start.3 = (bf16[1,2,256,384]{3,2,1,0:T(8,128)(2,1)S(1)}, bf16[1,2,256,384]{3,2,1,0:T(8,128)(2,1)}, u32[]{:S(2)}) copy-start(bf16[1,2,256,384]{3,2,1,0:T(8,128)(2,1)} %param.17) | copy-start | bytes 1179652
  0.7 11.9 %copy-start.4 = (bf16[1,2,256,384]{3,2,1,0:T(8,128)(2,1)S(1)}, bf16[1,2,256,384]{3,2,1,0:T(8,128)(2,1)}, u32[]{:S(2)}) copy-start(bf16[1,2,256,384]{3,2,1,0:T(8,128)(2,1)} %param.16) | copy-start | bytes 1179652
  0.7 11.9 %copy-start.5 = (bf16[1,2,256,384]{3,2,1,0:T(8,128)(2,1)S(1)}, bf16[1,2,256,384]{3,2,1,0:T(8,128)(2,1)}, u32[]{:S(2)}) copy-start(bf16[1,2,256,384]{3,2,1,0:T(8,128)(2,1)} %param.15) | copy-start | bytes 1179652
  244.0 4.5 %copy-start.2 = (bf16[3,2,16,16,384]{4,3,2,1,0:T(8,128)(2,1)S(1)}, bf16[3,2,16,16,384]{4,3,2,1,0:T(8,128)(2,1)}, u32[]{:S(2)}) copy-start(bf16[3,2,16,16,384]{4,3,2,1,0:T(8,128)(2,1)} %get-tuple-element.14) | copy-start | bytes 3538948
  248.5 1.1 copy-start.1
  248.5 1.2 copy-start.6

commit v4 on v3

--- a/solution.py
+++ b/solution.py
@@ -18,6 +18,7 @@
 RING = 8
 PEERS = 16
 CAP = 10
+TOP = 8
 BLOCK = RING * CAP
 SLOTS = PEERS * BLOCK
 TOK = 128
@@ -67,14 +68,14 @@
 
 
 def layer_kernel(
-    xa_ref, cb_ref, state, lookup,
-    out_a, out_b, grad_ref, fin_w, fin_m,
-    xall, call, code_a, code_b, gate, xs, cs, xr, sr,
+    xa_ref, cb_ref, table_ref, state, lookup,
+    out_rows, out_gates, grad_ref, fin_w, fin_m,
+    xall, call, table_a, table_b, code_a, code_b, gate, xs, cs, xr, sr,
     here, both, slots, run_m, got_m, out_m,
     wts, hg_hi, hg_lo, act_ref, hid, ag, hid_b,
-    pay_a, pay_b, back_a, back_b,
+    pay_a, pay_b, pay_g, back_a, back_b, back_g, gate_rows, gate_lanes,
     run_a, run_b, got_a, got_b, grads, grad_run, grad_got,
-    ag_send, ag_recv, out_send, out_recv, home_send, home_recv, rs_send, rs_recv,
+    ag_send, ag_recv, tb_send, tb_recv, out_send, out_recv, home_send, home_recv, hg_send, hg_recv, rs_send, rs_recv,
     mig_send, mig_recv, mig_local, mr_send, mr_recv, wt_send, wt_recv, gr_send, gr_recv, local,
 ):
     dp, y, z, core = place()
@@ -124,6 +125,24 @@
 
     def sent(step, way, half):
         return step < 3 or way == half
+
+    def table_piece(ring, way, step, arriving=False):
+        own, everyone, at, device = rings[ring]
+        everyone = (table_a, table_b)[ring]
+        sign = 1 if way == 0 else RING - 1
+        back = step + 1 if arriving else step
+        source = lax.rem(at + (RING - sign) * back, RING)
+        return pltpu.make_async_remote_copy(
+            src_ref=table_ref if step == 0 or arriving else everyone.at[source],
+            dst_ref=everyone.at[source],
+            send_sem=tb_send.at[ring, way, step],
+            recv_sem=tb_recv.at[ring, way, step],
+            device_id=device(lax.rem(at + sign, RING)),
+            device_id_type=MESH,
+        )
+
+    def table_sent(step, way):
+        return step < 3 or way == 0
 
     mig_device = (col_of, row_of)
     mig_mine = (col_mine, row_mine)
@@ -296,6 +315,12 @@
             weight_piece(way, 1, way).start()
 
     for step in range(4):
+        for ring in range(2):
+            for way in range(2):
+                if step > 0:
+                    table_piece(ring, way, step - 1, True).wait_recv()
+                if table_sent(step, way):
+                    table_piece(ring, way, step).start()
         for half in range(2):
             for ring in range(2):
                 for way in range(2):
@@ -307,6 +332,7 @@
             for ring in range(2):
                 own, everyone, at, device = rings[ring]
                 everyone[at] = own[...]
+                (table_a, table_b)[ring][at] = table_ref[...]
         if step == 0:
             mig_start(0)
         elif step == 1:
@@ -318,15 +344,38 @@
         for way in range(2):
             piece(ring, way, 3, way, True).wait_recv()
 
-    for source in range(RING):
-        lanes = pl.ds(source * TOK, TOK)
-        rows_a = pl.ds(pl.multiple_of(y * PEERS, PEERS), PEERS)
-        rows_b = pl.ds(pl.multiple_of(z * PEERS, PEERS), PEERS)
-        rank_a = xall[source, rows_a, D : D + TOK].astype(F32)
-        rank_b = call[source, rows_b, D : D + TOK].astype(F32)
-        code_a[:, lanes] = jnp.where(rank_a < 0, -1.0, rank_a + source * CAP)
-        code_b[:, lanes] = jnp.where(rank_b < 0, -1.0, rank_b + source * CAP)
-        gate[:, lanes] = call[source, rows_b, D + TOK :].astype(F32)
+    for ring in range(2):
+        table_piece(ring, 0, 3, True).wait_recv()
+    shape = (PEERS, TOK)
+    line = lax.broadcasted_iota(jnp.int32, shape, 0)
+    before = jnp.where(
+        lax.broadcasted_iota(jnp.int32, (TOK, TOK), 0) < lax.broadcasted_iota(jnp.int32, (TOK, TOK), 1),
+        1.0, 0.0,
+    ).astype(BF)
+    experts = (y * PEERS + line, (line // 2) * PEERS + z * 2 + lax.rem(line, 2))
+    for path in range(2):
+        expert = experts[path].astype(F32)
+        picked = []
+        for source in range(RING):
+            named = (table_a, table_b)[path][source].astype(F32)
+            chosen = jnp.zeros(shape, F32)
+            weight = jnp.zeros(shape, F32)
+            for k in range(TOP):
+                hit = expert == named[k : k + 1]
+                chosen = jnp.where(hit, 1.0, chosen)
+                if path == 1:
+                    weight = jnp.where(hit, named[TOP + k : TOP + k + 1], weight)
+            picked.append(chosen)
+            if path == 1:
+                gate[:, source * TOK : (source + 1) * TOK] = weight
+        ranks = jnp.dot(
+            jnp.concatenate(picked, axis=0).astype(BF), before, preferred_element_type=F32
+        )
+        for source in range(RING):
+            rank = ranks[source * PEERS : (source + 1) * PEERS]
+            (code_a, code_b)[path][:, source * TOK : (source + 1) * TOK] = jnp.where(
+                picked[source] > 0, rank + source * CAP, -1.0
+            )
 
     def exchange(path, slot_here, slot_there, peer):
         src, dst, device = ((xs, xr, row_of), (cs, sr, col_of))[path]
@@ -355,7 +404,7 @@
                 hots.append(one_hot_block(code_b[line, :], gate[line, :]))
         hot = jnp.concatenate(hots, axis=0)
         source = (xall, call)[path]
-        table = source[:, :, :D].reshape(RING * TOK, D)
+        table = source[...].reshape(RING * TOK, D)
         rows = jnp.dot(hot, table, preferred_element_type=F32).astype(BF)
         buffer = (xs, cs)[path]
         buffer[pl.ds(first, group)] = rows.reshape(group, BLOCK, D)
@@ -381,7 +430,6 @@
     mig_gather(4)
     mig_place()
     mig_start(1)
-    mig_start(2)
     for step in range(n_group):
         for path in range(2):
             if step > 1:
@@ -390,6 +438,7 @@
         if step == 2:
             mig_wait(1)
             weights_out()
+    mig_start(2)
     own_a = pltpu.make_async_copy(xs.at[row_mine], xr.at[row_mine], local.at[0])
     own_b = pltpu.make_async_copy(cs.at[col_mine], sr.at[col_mine], local.at[1])
     own_a.start()
@@ -448,6 +497,16 @@
             device_id_type=MESH,
         )
 
+    def gate_home(slot_here, slot_there, peer):
+        return pltpu.make_async_remote_copy(
+            src_ref=pay_g.at[slot_here],
+            dst_ref=back_g.at[slot_there],
+            send_sem=hg_send.at[slot_here],
+            recv_sem=hg_recv.at[slot_there],
+            device_id=row_of(peer),
+            device_id_type=MESH,
+        )
+
     def send_home(path, first):
         for k in range(group):
             peer = first + k
@@ -455,6 +514,8 @@
             @pl.when(peer != mines[path])
             def _():
                 home(path, peer, mines[path], peer).start()
+                if path == 0:
+                    gate_home(peer, row_mine, peer).start()
 
     def swaps(first):
         return jnp.concatenate([swap_block(first + k) for k in range(group)], axis=0)
@@ -472,19 +533,27 @@
         sigma = jax.nn.sigmoid(act)
         hidden = (act * sigma).astype(BF)
         act_grad = (hg * sigma * (1.0 + act * (1.0 - sigma))).astype(BF)
-        gates = jnp.sum(hg * hidden.astype(F32), axis=1, keepdims=True)
+        share = hg * hidden.astype(F32)
+        high = share.astype(BF)
+        low = (share - high.astype(F32)).astype(BF)
+        gates = jnp.zeros((16, group * TOK), F32)
+        for part in (high, low):
+            spread = []
+            for k in range(group):
+                spread += [part[k * BLOCK : (k + 1) * BLOCK], jnp.zeros((TOK - BLOCK, FF), BF)]
+            gates = gates + lax.dot_general(
+                jnp.ones((16, FF), BF), jnp.concatenate(spread, axis=0), (((1,), (1,)), ((), ())),
+                preferred_element_type=F32,
+            )
+        for k in range(group):
+            pay_g[first + k] = gates[:, k * TOK : (k + 1) * TOK].astype(BF)
         hid[rows, :] = hidden
         ag[rows, :] = act_grad
         pair = lax.dot_general(
             act_grad, up[0:2].reshape(width_a, FF), (((1,), (1,)), ((), ())),
             preferred_element_type=F32,
         )
-        lane = lax.broadcasted_iota(jnp.int32, (rows_per, TOK), 1)
-        here = pl.ds(first, group)
-        pay_a[here, :, :width_a] = pair.astype(BF).reshape(group, BLOCK, width_a)
-        pay_a[here, :, width_a:] = (
-            jnp.where(lane == me, gates, 0.0).astype(BF).reshape(group, BLOCK, TOK)
-        )
+        pay_a[pl.ds(first, group)] = pair.astype(BF).reshape(group, BLOCK, width_a)
         send_home(0, first)
 
     for step in range(n_group):
@@ -551,12 +620,34 @@
             peer = lax.rem(mines[path] + step, PEERS)
             home(path, peer, mines[path], peer).wait_send()
             home(path, mines[path], peer, peer).wait_recv()
+            if path == 0:
+                gate_home(peer, row_mine, peer).wait_send()
+                gate_home(row_mine, peer, peer).wait_recv()
             exchange(path, peer, mines[path], peer).wait_send()
         return carry
 
     lax.fori_loop(1, PEERS, finish, 0)
     own_a.wait()
     own_b.wait()
+
+    back_g[row_mine] = pay_g[row_mine]
+    own_line = lax.broadcasted_iota(jnp.int32, (PEERS, TOK), 0)
+    by_peer = jnp.zeros((PEERS, TOK), F32)
+    for k in range(PEERS):
+        by_peer = jnp.where(own_line == k, back_g[k].astype(F32), by_peer)
+    gate_rows[...] = jnp.zeros(gate_rows.shape, BF)
+    gate_rows[pl.ds(pl.multiple_of(y * PEERS, PEERS), PEERS)] = by_peer.astype(BF)
+    eye = jnp.where(
+        lax.broadcasted_iota(jnp.int32, (BLOCK, TOK), 0)
+        == lax.broadcasted_iota(jnp.int32, (BLOCK, TOK), 1),
+        1.0, 0.0,
+    ).astype(BF)
+    by_slot = lax.dot_general(
+        eye, gate_rows[...], (((1,), (1,)), ((), ())), preferred_element_type=F32
+    )
+    lane = lax.broadcasted_iota(jnp.int32, (BLOCK, TOK), 1)
+    for k in range(PEERS):
+        gate_lanes[k] = jnp.where(lane == y * PEERS + k, by_slot, 0.0).astype(BF)
 
     def combine(path, owner):
         code = (code_a, code_b)[path]
@@ -570,11 +661,20 @@
             ],
             axis=0,
         )
-        width = (LANES_A, LANES_B)[path]
-        return lax.dot_general(
-            hot, back[...].reshape(SLOTS, width), over_rows, preferred_element_type=F32
-        )
-
+        dot = functools.partial(
+            lax.dot_general, dimension_numbers=over_rows, preferred_element_type=F32
+        )
+        into = (xall, call)[path]
+        into[owner, :, :LANES_B] = dot(hot, back[...].reshape(SLOTS, LANES_B)).astype(BF)
+        if path == 0:
+            gated = dot(hot, gate_lanes[...].reshape(SLOTS, TOK))
+            into[owner, :, LANES_B:LANES_A] = gated.astype(BF)
+
+    for step in range(4):
+        for ring in range(2):
+            for way in range(2):
+                if table_sent(step, way):
+                    table_piece(ring, way, step).wait_send()
     for step in range(4):
         for ring in range(2):
             for way in range(2):
@@ -583,8 +683,8 @@
                         piece(ring, way, step, half).wait_send()
 
     def sums(owner, carry):
-        xall[owner, :, :LANES_A] = combine(0, owner).astype(BF)
-        call[owner, :, :LANES_B] = combine(1, owner).astype(BF)
+        combine(0, owner)
+        combine(1, owner)
         return carry
 
     lax.fori_loop(0, RING, sums, 0)
@@ -641,7 +741,12 @@
             for way in range(2):
                 hop(ring, way, 3, half).wait_recv()
                 total = total + got[way, 3, rows].astype(F32)
-            (out_a, out_b)[ring][rows] = total.astype(BF)
+            total = total.astype(BF)
+            if ring == 0:
+                out_rows[rows, :width_a] = total[:, :width_a]
+                out_gates[rows] = total[:, width_a:]
+            else:
+                out_rows[rows, width_a:] = total
 
     mig_end()
     for step in range(4):
@@ -657,7 +762,7 @@
         grad_hop(way, 0, way).wait_send()
 
 
-def layer(xa, cb, state, lookup):
+def layer(xa, cb, table, state, lookup):
     vm = pl.BlockSpec(memory_space=pltpu.VMEM)
     sm = pl.BlockSpec(memory_space=pltpu.SMEM)
     hbm = pl.BlockSpec(memory_space=pl.ANY)
@@ -668,17 +773,19 @@
     return pl.pallas_call(
         layer_kernel,
         out_shape=[
-            shape((TOK, LANES_A), BF),
-            shape((TOK, LANES_B), BF),
+            shape((TOK, D), BF),
+            shape((TOK, TOK), BF),
             shape((2, D // n_dp, FF), F32),
             shape((1, 2, PEERS, 16, FF), BF),
             shape((3, 2, PEERS, 16, FF), BF),
         ],
-        in_specs=[vm, vm, hbm, sm],
+        in_specs=[vm, vm, vm, hbm, sm],
         out_specs=[vm] * 4 + [hbm],
         scratch_shapes=[
-            pltpu.VMEM((RING, TOK, xa.shape[1]), BF),
-            pltpu.VMEM((RING, TOK, cb.shape[1]), BF),
+            pltpu.VMEM((RING, TOK, D), BF),
+            pltpu.VMEM((RING, TOK, D), BF),
+            pltpu.VMEM((RING, 2 * TOP, TOK), BF),
+            pltpu.VMEM((RING, 2 * TOP, TOK), BF),
             pltpu.VMEM((PEERS, RING * TOK), F32),
             pltpu.VMEM((PEERS, RING * TOK), F32),
             pltpu.VMEM((PEERS, RING * TOK), F32),
@@ -703,10 +810,14 @@
             pltpu.VMEM((SLOTS, FF), BF),
             pltpu.VMEM((SLOTS, FF), BF),
             pltpu.VMEM((SLOTS, FF), BF),
-            pltpu.VMEM((PEERS, BLOCK, LANES_A), BF),
             pltpu.VMEM((PEERS, BLOCK, LANES_B), BF),
-            pltpu.VMEM((PEERS, BLOCK, LANES_A), BF),
             pltpu.VMEM((PEERS, BLOCK, LANES_B), BF),
+            pltpu.VMEM((PEERS, 16, TOK), BF),
+            pltpu.VMEM((PEERS, BLOCK, LANES_B), BF),
+            pltpu.VMEM((PEERS, BLOCK, LANES_B), BF),
+            pltpu.VMEM((PEERS, 16, TOK), BF),
+            pltpu.VMEM((TOK, TOK), BF),
+            pltpu.VMEM((PEERS, BLOCK, TOK), BF),
             pltpu.VMEM((2, 4, TOK, LANES_A), BF),
             pltpu.VMEM((2, 4, TOK, LANES_B), BF),
             pltpu.VMEM((2, 4, TOK, LANES_A), BF),
@@ -716,10 +827,14 @@
             pltpu.VMEM((2, 2, 2, D // n_dp, FF), BF),
             dma((2, 2, 4, 2)),
             dma((2, 2, 4, 2)),
+            dma((2, 2, 4)),
+            dma((2, 2, 4)),
             dma((2, PEERS)),
             dma((2, PEERS)),
             dma((2, PEERS)),
             dma((2, PEERS)),
+            dma((PEERS,)),
+            dma((PEERS,)),
             dma((2, 2, 4, 2)),
             dma((2, 2, 4, 2)),
             dma((2, 3, PEERS)),
@@ -737,7 +852,7 @@
             collective_id=0, has_side_effects=True, vmem_limit_bytes=62 * 2**20
         ),
         name="layer",
-    )(xa, cb, state, lookup)
+    )(xa, cb, table, state, lookup)
 
 
 def moved(plan, index):
@@ -786,27 +901,15 @@
     put_down = source(y * PEERS + spot)
     lookup = jnp.stack([take_up, take_down, put_up, put_down])
 
-    columns = jnp.arange(count, dtype=jnp.int32)
-    hits = columns[:, None, None] == target.T[None]
-    chosen = jnp.any(hits, axis=1)
-    gates = jnp.sum(jnp.where(hits, gate_weights.T[None], 0), axis=1).astype(BF)
-    before = (jnp.arange(TOK)[:, None] < jnp.arange(TOK)[None, :]).astype(BF)
-    rank = jnp.dot(chosen.astype(BF), before, preferred_element_type=F32)
-    rank = jnp.where(chosen, rank, -1.0).astype(BF)
-
-    def by_column(table):
-        return table.reshape(RING, RING, 2, TOK).transpose(1, 0, 2, 3).reshape(count, TOK)
-
-    xa = jnp.concatenate([tokens, rank], axis=1)
-    cb = jnp.concatenate([cotangent, by_column(rank), by_column(gates)], axis=1)
-    sum_a, sum_b, grad, weights, moments = layer(xa, cb, state, lookup)
+    table = jnp.concatenate([target.T.astype(BF), gate_weights.T])
+    token_grad, gate_sums, grad, weights, moments = layer(tokens, cotangent, table, state, lookup)
     weights = weights.reshape(shape)
     moment_one, moment_two, average = (moments[k].reshape(shape) for k in range(3))
     master = jnp.where(stays, master, weights.astype(F32))
     grad = grad[None]
     new_master, first, second, smooth = adam_update(master, moment_one, moment_two, average, grad)
-    token_grad = jnp.concatenate([sum_a[:, : LANES_A - TOK], sum_b], axis=1)
-    gate_sums = sum_a[:, LANES_A - TOK :].astype(F32)
+    columns = jnp.arange(count, dtype=jnp.int32)
+    gate_sums = gate_sums.astype(F32)
     picked = jnp.sum(
         jnp.where(target[:, :, None] == columns[None, None, :], gate_sums[:, None, :], 0.0), axis=2
     )

time: 253 us -> 240 us (0.949)
  Pallas kernels: 230 us -> 219 us
    pallas_call x1, Pallas kernels: 230 us -> 219 us  [layer(): pl.pallas_call(layer_kernel, out_shape=[shape((TOK, D), BF), shape((TOK,...]
    concatenate x3 -> x1, other arithmetic: 5.01 us -> 1.27 us  [shards(): table = jnp.concatenate([target.T.astype(BF), gate_weights.T])]
where the time goes in v4:
time: 240 us; the launch traced here: 237 us
  Pallas kernels  219 us (91%)
  other arithmetic  13.1 us (5%)
  local copies, waits for them, and re-layouts  4.13 us (2%)
    pallas_call x1, Pallas kernels, layer(): pl.pallas_call(layer_kernel, out_shape=[shape((TOK, D), BF), shape((TOK,...  219 us

profile of v4, /device:TPU:1, one launch (start us, length us, event | category | flops | bytes accessed | tf_op | source)
XLA Modules:
  0.0 237.4 jit_solution(5921398149107925343)
XLA Ops:
  0.6 0.0 copy-start.2
  0.6 0.0 copy-start.3
  0.7 0.0 copy-start.4
  0.7 1.4 fusion.3
  2.8 0.8 slice_bitcast_fusion.1
  3.5 0.1 add_reduce_fusion.2
  3.6 0.8 add_reduce_fusion
  4.4 0.7 convert_bitcast_fusion.2
  5.1 1.3 pad_maximum_fusion.1.table_ref
  6.4 0.8 copy.23
  7.1 0.1 reshape.365
  7.2 0.1 eq.176
  7.3 0.2 select_reduce_fusion.2
  7.6 0.6 pad_add_fusion.lookup
  8.1 0.1 copy.25
  8.2 0.8 copy.26
  9.0 1.2 convert_element_type.75
  10.2 0.0 copy-done.2
  10.2 0.0 copy-done.3
  10.2 0.0 copy-done.4
  10.2 1.4 pad_maximum_fusion.state
  11.6 218.7 %layer.1 = (bf16[128,1024]{1,0:T(8,128)(2,1)}, bf16[128,128]{1,0:T(8,128)(2,1)}, f32[2,256,384]{2,1,0:T(8,128)}, bf16[1,2,16,16,384]{4,3,2,1,0:T(8,128)(2,1)}, bf16[3,2,16,16,384]{4,3,2,1,0:T(8,128)(2,1)}) custom-call(bf16[128,1024]{1,0:T(8,128)(2,1)} %xa_ref.1, bf16[128,1024]{1,0:T(8,128)(2,1)} %cb_ref.1, bf16[16,128]{1,0:T(8,128)(2,1)} %pad_maximum_fusion.1.table_ref, ...), custom_call_target="tpu_custom_call" | custom-call | tf_op jit(solution)/shard_map/layer/pallas_call | solution.py:773
  230.4 0.8 convert_element_type.76
  231.1 0.4 select_reduce_fusion
  231.5 0.7 copy.27
  232.2 0.0 copy-start
  232.2 0.0 copy-start.1
  232.2 0.0 copy-start.5
  232.2 1.6 convert_multiply_fusion.2
  233.8 0.0 copy-done
  233.8 0.1 copy-done.1
  233.9 0.1 copy-done.5
  234.0 1.6 fusion.2
  235.6 0.0 copy-start.6
  235.6 1.1 convert_bitcast_fusion
  236.7 0.0 copy-done.6
  236.7 0.7 copy.29
  (8 shorter events, 0.1 us)
Async XLA Ops:
  0.6 9.6 %copy-start.2 = (bf16[1,2,256,384]{3,2,1,0:T(8,128)(2,1)S(1)}, bf16[1,2,256,384]{3,2,1,0:T(8,128)(2,1)}, u32[]{:S(2)}) copy-start(bf16[1,2,256,384]{3,2,1,0:T(8,128)(2,1)} %param.17) | copy-start | bytes 1179652
  0.6 9.6 %copy-start.3 = (bf16[1,2,256,384]{3,2,1,0:T(8,128)(2,1)S(1)}, bf16[1,2,256,384]{3,2,1,0:T(8,128)(2,1)}, u32[]{:S(2)}) copy-start(bf16[1,2,256,384]{3,2,1,0:T(8,128)(2,1)} %param.16) | copy-start | bytes 1179652
  0.7 9.6 %copy-start.4 = (bf16[1,2,256,384]{3,2,1,0:T(8,128)(2,1)S(1)}, bf16[1,2,256,384]{3,2,1,0:T(8,128)(2,1)}, u32[]{:S(2)}) copy-start(bf16[1,2,256,384]{3,2,1,0:T(8,128)(2,1)} %param.15) | copy-start | bytes 1179652
  232.2 1.6 copy-start
  232.2 1.7 copy-start.1
  232.2 1.8 copy-start.5
  235.6 1.1 copy-start.6

commit v5 on v4

--- a/solution.py
+++ b/solution.py
@@ -68,9 +68,9 @@
 
 
 def layer_kernel(
-    xa_ref, cb_ref, table_ref, state, lookup,
+    xa_ref, cb_ref, ids_ref, gates_ref, state, plan, lookup,
     out_rows, out_gates, grad_ref, fin_w, fin_m,
-    xall, call, table_a, table_b, code_a, code_b, gate, xs, cs, xr, sr,
+    table_ref, gate_sums, xall, call, table_a, table_b, code_a, code_b, gate, xs, cs, xr, sr,
     here, both, slots, run_m, got_m, out_m,
     wts, hg_hi, hg_lo, act_ref, hid, ag, hid_b,
     pay_a, pay_b, pay_g, back_a, back_b, back_g, gate_rows, gate_lanes,
@@ -100,6 +100,14 @@
     lax.fori_loop(1, PEERS, signal, 0)
     for other in (x_right, x_left):
         pl.semaphore_signal(barrier, inc=1, device_id=(me, other), device_id_type=MESH)
+    named = ids_ref[...]
+    target = named
+    for i in range(plan.shape[0]):
+        one, other = plan[i, 0], plan[i, 1]
+        target = jnp.where(named == one, other, jnp.where(named == other, one, target))
+    table_ref[...] = jnp.concatenate(
+        [target.astype(F32), gates_ref[...].astype(F32)], axis=0
+    ).astype(BF)
     pl.semaphore_wait(barrier, 2 * (PEERS - 1) + 2)
 
     rings = (
@@ -682,13 +690,6 @@
                     if sent(step, way, half):
                         piece(ring, way, step, half).wait_send()
 
-    def sums(owner, carry):
-        combine(0, owner)
-        combine(1, owner)
-        return carry
-
-    lax.fori_loop(0, RING, sums, 0)
-
     loops = (
         (xall, run_a, got_a, y, lambda v: (v * PEERS + z * 2 + core, dp)),
         (call, run_b, got_b, z, lambda v: (y * PEERS + v * 2 + core, dp)),
@@ -711,6 +712,11 @@
         )
 
     for step in range(4):
+        for ring in range(2):
+            at = loops[ring][3]
+            combine(ring, lax.rem(at + 4 - step, RING))
+            if step > 0:
+                combine(ring, lax.rem(at + 4 + step, RING))
         for half in range(2):
             for ring in range(2):
                 part, run, got, at, device = loops[ring]
@@ -733,6 +739,8 @@
                     grad_hop(way, 1, half).wait_recv()
                     total = total + grad_got[way, 1, half].astype(F32)
                 grad_ref[half] = total
+    for ring in range(2):
+        combine(ring, loops[ring][3])
     for half in range(2):
         for ring in range(2):
             part, run, got, at, device = loops[ring]
@@ -744,10 +752,24 @@
             total = total.astype(BF)
             if ring == 0:
                 out_rows[rows, :width_a] = total[:, :width_a]
-                out_gates[rows] = total[:, width_a:]
+                gate_sums[rows] = total[:, width_a:]
             else:
                 out_rows[rows, width_a:] = total
 
+    square = lax.broadcasted_iota(jnp.int32, (TOK, TOK), 0)
+    turn = jnp.where(square == lax.broadcasted_iota(jnp.int32, (TOK, TOK), 1), 1.0, 0.0).astype(BF)
+    by_expert = lax.dot_general(
+        gate_sums[...], turn, (((0,), (0,)), ((), ())), preferred_element_type=F32
+    )
+    mine_named = table_ref[...].astype(F32)
+    chosen_sums = [
+        jnp.sum(
+            jnp.where(square.astype(F32) == mine_named[k : k + 1], by_expert, 0.0),
+            axis=0, keepdims=True,
+        )
+        for k in range(TOP)
+    ]
+    out_gates[...] = jnp.concatenate(chosen_sums, axis=0) / mine_named[TOP:]
     mig_end()
     for step in range(4):
         for ring in range(2):
@@ -762,7 +784,7 @@
         grad_hop(way, 0, way).wait_send()
 
 
-def layer(xa, cb, table, state, lookup):
+def layer(xa, cb, ids, gates, state, plan, lookup):
     vm = pl.BlockSpec(memory_space=pltpu.VMEM)
     sm = pl.BlockSpec(memory_space=pltpu.SMEM)
     hbm = pl.BlockSpec(memory_space=pl.ANY)
@@ -774,14 +796,16 @@
         layer_kernel,
         out_shape=[
             shape((TOK, D), BF),
-            shape((TOK, TOK), BF),
+            shape((TOP, TOK), F32),
             shape((2, D // n_dp, FF), F32),
             shape((1, 2, PEERS, 16, FF), BF),
             shape((3, 2, PEERS, 16, FF), BF),
         ],
-        in_specs=[vm, vm, vm, hbm, sm],
+        in_specs=[vm, vm, vm, vm, hbm, sm, sm],
         out_specs=[vm] * 4 + [hbm],
         scratch_shapes=[
+            pltpu.VMEM((2 * TOP, TOK), BF),
+            pltpu.VMEM((TOK, TOK), BF),
             pltpu.VMEM((RING, TOK, D), BF),
             pltpu.VMEM((RING, TOK, D), BF),
             pltpu.VMEM((RING, 2 * TOP, TOK), BF),
@@ -852,7 +876,7 @@
             collective_id=0, has_side_effects=True, vmem_limit_bytes=62 * 2**20
         ),
         name="layer",
-    )(xa, cb, table, state, lookup)
+    )(xa, cb, ids, gates, state, plan, lookup)
 
 
 def moved(plan, index):
@@ -875,9 +899,7 @@
     tokens, expert_ids, gate_weights, cotangent, migration_plan,
     master, moment_one, moment_two, average,
 ):
-    count = lax.axis_size("ep")
     me = lax.axis_index("ep")
-    target = moved(migration_plan, expert_ids)
 
     shape = master.shape
     state = jnp.stack(
@@ -901,19 +923,15 @@
     put_down = source(y * PEERS + spot)
     lookup = jnp.stack([take_up, take_down, put_up, put_down])
 
-    table = jnp.concatenate([target.T.astype(BF), gate_weights.T])
-    token_grad, gate_sums, grad, weights, moments = layer(tokens, cotangent, table, state, lookup)
+    token_grad, gate_grad, grad, weights, moments = layer(
+        tokens, cotangent, expert_ids.T, gate_weights.T, state, migration_plan, lookup
+    )
     weights = weights.reshape(shape)
     moment_one, moment_two, average = (moments[k].reshape(shape) for k in range(3))
     master = jnp.where(stays, master, weights.astype(F32))
     grad = grad[None]
     new_master, first, second, smooth = adam_update(master, moment_one, moment_two, average, grad)
-    columns = jnp.arange(count, dtype=jnp.int32)
-    gate_sums = gate_sums.astype(F32)
-    picked = jnp.sum(
-        jnp.where(target[:, :, None] == columns[None, None, :], gate_sums[:, None, :], 0.0), axis=2
-    )
-    gate_grad = (picked / gate_weights.astype(F32)).astype(BF)
+    gate_grad = gate_grad.T.astype(BF)
     return (token_grad, gate_grad, new_master, first, second, smooth)
 
 

time: 240 us -> 232 us (0.967)
  Pallas kernels: 219 us -> 215 us
  other arithmetic: 13.1 us -> 10.5 us
    pallas_call x1, Pallas kernels: 219 us -> 215 us  [layer(): pl.pallas_call(layer_kernel, out_shape=[shape((TOK, D), BF), shape((TOP,...]
where the time goes in v5:
time: 232 us; the launch traced here: 230 us
  Pallas kernels  215 us (93%)
  other arithmetic  10.5 us (5%)
  local copies, waits for them, and re-layouts  2.59 us (1%)
    pallas_call x1, Pallas kernels, layer(): pl.pallas_call(layer_kernel, out_shape=[shape((TOK, D), BF), shape((TOP,...  215 us

profile of v5, /device:TPU:1, one launch (start us, length us, event | category | flops | bytes accessed | tf_op | source)
XLA Modules:
  0.0 229.6 jit_solution(9269133109694176546)
XLA Ops:
  0.6 0.0 copy-start.2
  0.6 0.0 copy-start.3
  0.7 0.0 copy-start.4
  0.7 1.4 fusion.3
  2.8 0.8 slice_bitcast_fusion.1
  3.5 0.1 add_reduce_fusion.1
  3.6 0.8 copy.23.plan
  4.4 0.0 copy-start.7
  4.4 0.1 reshape.360
  4.5 0.1 eq.137
  4.6 0.2 select_reduce_fusion.1
  4.8 0.6 pad_add_fusion.lookup
  5.4 1.2 convert_element_type.64
  6.6 0.0 copy-done.2
  6.6 0.0 copy-done.3
  6.6 0.0 copy-done.4
  6.6 1.4 pad_maximum_fusion.state
  8.0 0.0 copy-done.7
  8.0 215.1 %layer.1 = (bf16[128,1024]{1,0:T(8,128)(2,1)}, f32[8,128]{1,0:T(8,128)}, f32[2,256,384]{2,1,0:T(8,128)}, bf16[1,2,16,16,384]{4,3,2,1,0:T(8,128)(2,1)}, bf16[3,2,16,16,384]{4,3,2,1,0:T(8,128)(2,1)}) custom-call(bf16[128,1024]{1,0:T(8,128)(2,1)} %xa_ref.1, bf16[128,1024]{1,0:T(8,128)(2,1)} %cb_ref.1, s32[8,128]{1,0:T(8,128)} %bitcast.45, ...), custom_call_target="tpu_custom_call" | custom-call | tf_op jit(solution)/shard_map/layer/pallas_call | solution.py:795
  223.2 1.3 convert_bitcast_fusion.2
  224.4 0.0 copy-start
  224.4 0.0 copy-start.1
  224.4 0.0 copy-start.5
  224.4 1.6 convert_multiply_fusion.2
  226.0 0.0 copy-done
  226.1 0.1 copy-done.1
  226.1 0.1 copy-done.5
  226.2 1.6 fusion.2
  227.9 0.0 copy-start.6
  227.9 1.1 convert_bitcast_fusion
  228.9 0.0 copy-done.6
  228.9 0.7 copy.25
  (7 shorter events, 0.1 us)
Async XLA Ops:
  0.6 5.9 %copy-start.2 = (bf16[1,2,256,384]{3,2,1,0:T(8,128)(2,1)S(1)}, bf16[1,2,256,384]{3,2,1,0:T(8,128)(2,1)}, u32[]{:S(2)}) copy-start(bf16[1,2,256,384]{3,2,1,0:T(8,128)(2,1)} %param.17) | copy-start | bytes 1179652
  0.6 5.9 %copy-start.3 = (bf16[1,2,256,384]{3,2,1,0:T(8,128)(2,1)S(1)}, bf16[1,2,256,384]{3,2,1,0:T(8,128)(2,1)}, u32[]{:S(2)}) copy-start(bf16[1,2,256,384]{3,2,1,0:T(8,128)(2,1)} %param.16) | copy-start | bytes 1179652
  0.7 5.9 %copy-start.4 = (bf16[1,2,256,384]{3,2,1,0:T(8,128)(2,1)S(1)}, bf16[1,2,256,384]{3,2,1,0:T(8,128)(2,1)}, u32[]{:S(2)}) copy-start(bf16[1,2,256,384]{3,2,1,0:T(8,128)(2,1)} %param.15) | copy-start | bytes 1179652
  4.4 3.6 %copy-start.7 = (s32[8,2]{1,0:T(8,128)}, s32[8,2]{1,0:T(8,128)S(1)}, u32[]{:S(2)}) copy-start(s32[8,2]{1,0:T(8,128)S(1)} %copy.23.plan) | copy-start | bytes 196
  224.4 1.6 copy-start
  224.4 1.7 copy-start.1
  224.4 1.8 copy-start.5
  227.9 1.1 copy-start.6
